TPU v7x, 32 devices: a whole 2x2x4 slice. The times are simulated.
32 devices in a mesh: stream: 4 (over y, core), seq: 8 (over z, x).
Axes of the slice: x: 2, y: 2, z: 4, core: 2. Of those that a mesh axis runs over, the one named last changes fastest.
Arguments:
- step_codes: int32 [1024, 16, 64], P('seq', None, 'stream'), may hold values from 0 to 254, as said below
- segments: int32 [1024, 16], P('seq'), may hold values from 0 to 15, as said below
- embed_table: float32 [1297, 256], replicated, may hold values from -1.5 to 1.5
- qkv_weight: float32 [2, 256, 768], replicated, may hold values from -0.375 to 0.375
- square_weight: float32 [2, 2, 256, 256], replicated, may hold values from -1 to 1
- up_weight: float32 [2, 256, 1024], replicated, may hold values from -0.375 to 0.375
- down_weight: float32 [2, 1024, 256], replicated, may hold values from -0.1875 to 0.1875
- small_params: float32 [9, 256], replicated, may hold values from 0.5 to 1.5
- head_weight: float32 [256, 1280], replicated, may hold values from -0.375 to 0.375
- moment_table: float32 [1297, 256], replicated, may hold values from -5.722046e-06 to 5.722046e-06
- moment_qkv: float32 [2, 256, 768], replicated, may hold values from -5.722046e-06 to 5.722046e-06
- moment_square: float32 [2, 2, 256, 256], replicated, may hold values from -5.722046e-06 to 5.722046e-06
- moment_up: float32 [2, 256, 1024], replicated, may hold values from -5.722046e-06 to 5.722046e-06
- moment_down: float32 [2, 1024, 256], replicated, may hold values from -5.722046e-06 to 5.722046e-06
- moment_small: float32 [9, 256], replicated, may hold values from -1.9073486e-05 to 1.9073486e-05
- moment_head: float32 [256, 1280], replicated, may hold values from -5.722046e-06 to 5.722046e-06
- average_table: float32 [1297, 256], replicated, may hold values from -1.5 to 1.5
- average_qkv: float32 [2, 256, 768], replicated, may hold values from -0.375 to 0.375
- average_square: float32 [2, 2, 256, 256], replicated, may hold values from -1 to 1
- average_up: float32 [2, 256, 1024], replicated, may hold values from -0.375 to 0.375
- average_down: float32 [2, 1024, 256], replicated, may hold values from -0.1875 to 0.1875
- average_small: float32 [9, 256], replicated, may hold values from 0.5 to 1.5
- average_head: float32 [256, 1280], replicated, may hold values from -0.375 to 0.375
Outputs:
- loss_sum: float32 [], replicated
- term_count: float32 [], replicated
- grad_norm: float32 [], replicated
- new_table: float32 [1297, 256], replicated
- new_qkv: float32 [2, 256, 768], replicated
- new_square: float32 [2, 2, 256, 256], replicated
- new_up: float32 [2, 256, 1024], replicated
- new_down: float32 [2, 1024, 256], replicated
- new_small: float32 [9, 256], replicated
- new_head: float32 [256, 1280], replicated
- next_moment_table: float32 [1297, 256], replicated
- next_moment_qkv: float32 [2, 256, 768], replicated
- next_moment_square: float32 [2, 2, 256, 256], replicated
- next_moment_up: float32 [2, 256, 1024], replicated
- next_moment_down: float32 [2, 1024, 256], replicated
- next_moment_small: float32 [9, 256], replicated
- next_moment_head: float32 [256, 1280], replicated
- next_average_table: float32 [1297, 256], replicated
- next_average_qkv: float32 [2, 256, 768], replicated
- next_average_square: float32 [2, 2, 256, 256], replicated
- next_average_up: float32 [2, 256, 1024], replicated
- next_average_down: float32 [2, 1024, 256], replicated
- next_average_small: float32 [9, 256], replicated
- next_average_head: float32 [256, 1280], replicated
Inputs may be any that keep to these rules, and one draw needn't show every extreme that they name: `step_codes`: columns j < 32 hold latent codes below 32; column 32 an action below 18, column 33 a discount of 0 or 1, column 48 a reward class below 255; all other columns are 0. `segments`: each sequence's ids start at 0 and rise by 0 or 1 from step to step.
All inputs are finite; a program needn't handle non-finite values.
Results may differ from a plain program's by a relative error of at most 0.014.
Values may be sent and summed in bfloat16 or wider, within the bound.
A program may use at most 256 MiB of HBM per device.

v0:
```python
import math

import jax
import jax.numpy as jnp
import numpy as np
from jax import lax
from jax.experimental import pallas as pl
from jax.experimental.pallas import tpu as pltpu
from jax.sharding import PartitionSpec as P

D = 256
HEADS = 8
HD = 32
FF = 1024
CATS = 32
CLASSES = 32
NA = 18
STEPS = 16
TOKS = 48
HK = HEADS * TOKS
LAYERS = 2
HCOLS = 1280
TROWS = 1408
CHUNK = 8
EPSILON = 1e-06
MOMENTUM_RATE = 0.9
AVERAGE_RATE = 0.7
CLIP_SCALE = 0.2
STEP_SCALE = 0.03
MASKED = -1e30
POSITION_SCALE = 0.5
SCALE = HD ** (-0.5)
BF = jnp.bfloat16
F32 = jnp.float32
VMEM_LIMIT = 63 * 1000 * 1000


def dot_nn(a, b):
    return lax.dot_general(a, b, (((1,), (0,)), ((), ())), preferred_element_type=F32)


def dot_nt(a, b):
    return lax.dot_general(a, b, (((1,), (1,)), ((), ())), preferred_element_type=F32)


def dot_tn(a, b):
    return lax.dot_general(a, b, (((0,), (0,)), ((), ())), preferred_element_type=F32)


def iota(shape, dim):
    return lax.broadcasted_iota(jnp.int32, shape, dim)


def position_rows():
    distance = np.arange(TOKS, dtype=np.float32)[:, None]
    rates = np.exp(np.arange(D // 2, dtype=np.float32) * np.float32(-2.0 * math.log(10000.0) / D))
    angle = (distance * rates[None, :].astype(np.float32)).astype(np.float32)
    table = np.float32(POSITION_SCALE) * np.concatenate([np.sin(angle), np.cos(angle)], axis=1)
    rows = np.zeros((3, TOKS, D), np.float32)
    for i in range(3):
        for j in range(3):
            for e in range(STEPS):
                d = 3 * (STEPS - 1 - e) + i - j
                if d >= 0:
                    rows[i, j * STEPS + e] = table[d]
    return rows.reshape(3 * TOKS, D)


def rms(values):
    return lax.rsqrt(jnp.mean(values * values, axis=-1, keepdims=True) + EPSILON)


def head_mask(h, rows):
    lane = iota((rows, 128), 1)
    low = (h % 4) * HD
    return ((lane >= low) & (lane < low + HD)).astype(F32).astype(BF)


def expand(rows):
    zero = jnp.zeros((TOKS, 128), BF)
    parts = []
    for h in range(HEADS):
        half = rows[:, 128 * (h // 4) : 128 * (h // 4) + 128] * head_mask(h, TOKS)
        parts.append(jnp.concatenate([half, zero] if h < 4 else [zero, half], axis=1))
    return jnp.concatenate(parts, axis=0)


def fold(values):
    lane = iota((TOKS, 128), 1)
    halves = []
    for g in range(2):
        total = None
        for h in range(4):
            part = values[(4 * g + h) * TOKS : (4 * g + h + 1) * TOKS, 128 * g : 128 * g + 128]
            total = part if total is None else jnp.where(lane >= h * HD, part, total)
        halves.append(total)
    return jnp.concatenate(halves, axis=1)


def spans(tile):
    found = []
    for h in range(HEADS):
        low, high = max(TOKS * h - 128 * tile, 0), min(TOKS * (h + 1) - 128 * tile, 128)
        if low < high:
            found.append((h, low, high))
    return found


def segment_max(scores):
    rows = scores.shape[0]
    lane = iota((rows, 128), 1)
    tiles = [scores[:, 128 * t : 128 * t + 128] for t in range(3)]
    best = {}
    for t in range(3):
        for h, low, high in spans(t):
            part = jnp.where((lane >= low) & (lane < high), tiles[t], -3e38)
            best[h] = part if h not in best else jnp.maximum(best[h], part)
    best = {h: jnp.max(v, axis=1, keepdims=True) for h, v in best.items()}
    outs = []
    for t in range(3):
        total = None
        for h, low, high in spans(t):
            wide = jnp.broadcast_to(best[h], (rows, 128))
            total = wide if total is None else jnp.where(lane >= low, wide, total)
        outs.append(total)
    return jnp.concatenate(outs, axis=1)


def unskew(values):
    row = iota((STEPS, HK), 0)
    values = jnp.concatenate(
        [pltpu.roll(values[:8], 15, 1), pltpu.roll(values[8:], 7, 1)], axis=0
    )
    for bit in (1, 2, 4):
        values = jnp.where((row & bit) > 0, pltpu.roll(values, HK - bit, 1), values)
    return values


def compute_kernel(
    codes_ref,
    seg_ref,
    pos_ref,
    small_ref,
    table_ref,
    wqkv_ref,
    wsq_ref,
    wup_ref,
    wdown_ref,
    whead_ref,
    g_ref,
    e_ref,
    x_s,
    att_s,
    pu_s,
    r_s,
    o_s,
    mid_s,
    hb_s,
    gp_s,
    a_s,
    b_s,
    dyl_s,
    dml_s,
    dx_s,
    rk_s,
    start_s,
    l_s,
    slope_s,
):
    seqs = codes_ref.shape[1]
    steps_all = seqs * STEPS
    toks = seqs * TOKS
    chunks = seqs // CHUNK
    rows_c = CHUNK * TOKS

    seg = seg_ref[...].astype(F32)
    seg3 = jnp.broadcast_to(seg[:, None, :], (seqs, STEPS, STEPS))
    i1, i2 = iota((seqs, STEPS, STEPS), 1), iota((seqs, STEPS, STEPS), 2)
    seg_col = jnp.sum(jnp.where(i1 == i2, seg3, 0.0), axis=2, keepdims=True)
    start = jnp.sum(jnp.where(seg3 < seg_col, 1.0, 0.0), axis=2, keepdims=True)
    start_s[...] = jnp.broadcast_to(start, (seqs, STEPS, 128))
    follow = jnp.where((i2 == i1 + 1) & (seg3 == seg_col), 1.0, 0.0).reshape(steps_all, STEPS)
    valid_row = dot_nt(jnp.ones((8, STEPS), BF), follow.astype(BF))[:1]

    codes = [codes_ref[k].reshape(steps_all, STEPS).astype(F32) for k in range(4)]
    spread = (iota((STEPS, 512), 1) // CLASSES == iota((STEPS, 512), 0)).astype(F32).astype(BF)
    class_lane = (iota((128, 512), 1) % CLASSES).astype(F32)
    for c in range(steps_all // 128):
        rows = slice(128 * c, 128 * c + 128)
        seq_rows = slice(8 * c, 8 * c + 8)
        halves = []
        for k in range(2):
            hot = (dot_nn(codes[k][rows].astype(BF), spread) == class_lane).astype(F32).astype(BF)
            piece = dot_nn(hot, table_ref[512 * k : 512 * k + 512]).astype(BF).astype(F32)
            halves.append(piece)
        x_s[0, seq_rows, 0] = (halves[0] + halves[1]).reshape(8, STEPS, D)
        lane = iota((128, 128), 1).astype(F32)
        hot = (codes[2][rows, 0:1] == lane).astype(F32).astype(BF)
        x_s[0, seq_rows, 1] = (
            dot_nn(hot, table_ref[1024:1152]).astype(BF).astype(F32).reshape(8, STEPS, D)
        )
        lane = iota((128, 384), 1).astype(F32)
        hot = (codes[3][rows, 0:1] + NA == lane).astype(F32).astype(BF)
        x_s[0, seq_rows, 2] = (
            dot_nn(hot, table_ref[1024:1408]).astype(BF).astype(F32).reshape(8, STEPS, D)
        )

    for layer in range(LAYERS):
        rk = dot_nn(pos_ref[...], wsq_ref[layer, 1]).astype(BF)
        for k in range(3):
            rk_s[layer, k] = expand(rk[TOKS * k : TOKS * k + TOKS])

    lane_hk = iota((TOKS, HK), 1) % TOKS
    key_step = lane_hk % STEPS
    key_time = 3 * key_step + lane_hk // STEPS
    row_tok = iota((TOKS, HK), 0)
    query_time = 3 * (row_tok % STEPS) + row_tok // STEPS
    causal = key_time <= query_time
    key_step_f = key_step.astype(F32)
    sum_hd = (iota((HK, D), 0) // TOKS == iota((HK, D), 1) // HD).astype(F32).astype(BF)
    sum_hk = (iota((D, HK), 0) // HD == iota((D, HK), 1) // TOKS).astype(F32).astype(BF)

    for layer in range(LAYERS):
        gain_a = small_ref[4 * layer : 4 * layer + 1]
        gain_b = small_ref[4 * layer + 1 : 4 * layer + 2]
        bias_u = small_ref[4 * layer + 2 : 4 * layer + 3]
        bias_v = small_ref[4 * layer + 3 : 4 * layer + 4]

        @pl.loop(0, chunks)
        def _(c):
            rows = pl.ds(pl.multiple_of(c * rows_c, rows_c), rows_c)
            x = x_s[layer, pl.ds(c * CHUNK, CHUNK)].reshape(rows_c, D)
            low = (x * rms(x) * gain_a).astype(BF)
            a_s[layer, rows] = low
            q = dot_nn(low, wqkv_ref[layer, :, :256]).astype(BF).astype(F32)
            qu = (q + bias_u).astype(BF)
            qv = (q + bias_v).astype(BF)
            key = dot_nn(low, wqkv_ref[layer, :, 256:512]).astype(BF)
            val = dot_nn(low, wqkv_ref[layer, :, 512:]).astype(BF)
            att_s[layer, rows, 0:256] = qu
            att_s[layer, rows, 256:512] = qv
            att_s[layer, rows, 512:768] = key
            att_s[layer, rows, 768:1024] = val
            qv4 = qv.reshape(CHUNK, 3, STEPS, D)
            place = [
                dot_nt(qv4[:, k].reshape(CHUNK * STEPS, D), rk_s[layer, k]) for k in range(3)
            ]
            start_c = start_s[pl.ds(c * CHUNK, CHUNK)]
            for b in range(CHUNK):
                span = slice(TOKS * b, TOKS * b + TOKS)
                score = dot_nt(qu[span], expand(key[span]))
                shifted = [
                    pltpu.roll(
                        place[k][STEPS * b : STEPS * b + STEPS],
                        HK - (STEPS - 1),
                        1,
                        stride=1,
                        stride_axis=0,
                    )
                    for k in range(3)
                ]
                begin = jnp.concatenate([start_c[b]] * 3, axis=0)
                begin = jnp.concatenate([begin] * 3, axis=1)
                score = (score + jnp.concatenate(shifted, axis=0)) * SCALE
                score = jnp.where(causal & (key_step_f >= begin), score, MASKED)
                probs = jnp.exp(score - segment_max(score)).astype(BF)
                pu_s[layer, pl.ds(pl.multiple_of(c * rows_c + TOKS * b, TOKS), TOKS)] = probs
                l_s[span] = dot_nn(probs, expand(val[span]))
            recip = 1.0 / dot_nn(pu_s[layer, rows], sum_hd)
            out = l_s[...] * recip
            r_s[layer, rows] = recip
            o_s[layer, rows] = out
            mid = x + dot_nn(out.astype(BF), wsq_ref[layer, 0])
            mid_s[layer, rows] = mid
            low = (mid * rms(mid) * gain_b).astype(BF)
            b_s[layer, rows] = low
            for j in range(FF // 256):
                cols = slice(256 * j, 256 * j + 256)
                inner = dot_nn(low, wup_ref[layer, :, cols])
                square = inner * inner
                c0 = math.sqrt(2.0 / math.pi)
                tanh = jnp.tanh(c0 * inner * (1.0 + 0.044715 * square))
                half = 0.5 * (1.0 + tanh)
                hb_s[layer, rows, cols] = (inner * half).astype(BF)
                gp_s[layer, rows, cols] = (
                    half
                    + (0.5 * c0) * inner * (1.0 - tanh * tanh) * (1.0 + (3 * 0.044715) * square)
                ).astype(BF)
            nxt = mid + dot_nn(hb_s[layer, rows], wdown_ref[layer])
            x_s[layer + 1, pl.ds(c * CHUNK, CHUNK)] = nxt.reshape(CHUNK, 3, STEPS, D)

    gain_f = small_ref[4 * LAYERS : 4 * LAYERS + 1]
    xf = x_s[LAYERS, :, 1].reshape(steps_all, D)
    feat = (xf * rms(xf) * gain_f).astype(BF)
    spread_t = (iota((512, STEPS), 0) // CLASSES == iota((512, STEPS), 1)).astype(F32).astype(BF)
    class_row = iota((4, CLASSES, steps_all), 1).astype(F32)
    loss = jnp.zeros((4, steps_all), F32)
    for k in range(2):
        follow_codes = pltpu.roll(codes[k], steps_all - 1, 0).astype(BF)
        for j in range(4):
            base = 512 * k + 128 * j
            logits = dot_nt(whead_ref[base : base + 128], feat).reshape(4, CLASSES, steps_all)
            target = dot_nt(spread_t[128 * j : 128 * j + 128], follow_codes)
            hot = target.reshape(4, CLASSES, steps_all) == class_row
            top = jnp.max(logits, axis=1, keepdims=True)
            grown = jnp.exp(logits - top)
            total = jnp.sum(grown, axis=1, keepdims=True)
            picked = jnp.sum(jnp.where(hot, logits, 0.0), axis=1)
            loss = loss + valid_row * (jnp.log(total[:, 0]) + top[:, 0] - picked)
            slope = (grown * (1.0 / total) - jnp.where(hot, 1.0, 0.0)) * valid_row[None]
            slope_s[base : base + 128] = slope.reshape(128, steps_all).astype(BF)
    pick0 = (iota((8, STEPS), 1) == 0).astype(F32).astype(BF)
    pick1 = (iota((8, STEPS), 1) == 1).astype(F32).astype(BF)
    action_row = dot_nt(pick0, codes[2].astype(BF))[:1]
    discount_row = dot_nt(pick1, codes[2].astype(BF))[:1]
    reward_row = dot_nt(pick0, codes[3].astype(BF))[:1]
    logits = dot_nt(whead_ref[1024:1280], feat)
    row = iota((256, steps_all), 0)
    hot = row == (reward_row + 1.0).astype(jnp.int32)
    disc = logits[:1]
    masked = jnp.where(row == 0, -3e38, logits)
    top = jnp.max(masked, axis=0, keepdims=True)
    grown = jnp.exp(masked - top)
    total = jnp.sum(grown, axis=0, keepdims=True)
    picked = jnp.sum(jnp.where(hot, logits, 0.0), axis=0, keepdims=True)
    fade = jnp.exp(-jnp.abs(disc))
    soft = jnp.maximum(disc, 0.0) + jnp.log(1.0 + fade)
    sigm = jnp.where(disc >= 0.0, 1.0, fade) / (1.0 + fade)
    loss_row = (
        jnp.sum(loss, axis=0, keepdims=True)
        + jnp.log(total)
        + top
        - picked
        + soft
        - discount_row * disc
    )
    slope = grown * (1.0 / total) - jnp.where(hot, 1.0, 0.0)
    slope = jnp.where(row == 0, sigm - discount_row, slope)
    slope_s[1024:1280] = slope.astype(BF)
    loss_sum = jnp.sum(loss_row)
    count = jnp.sum(valid_row) * CATS + 2.0 * steps_all
    e_ref[9:10] = jnp.full((1, D), loss_sum, F32)
    e_ref[10:11] = jnp.full((1, D), count, F32)
    e_ref[11:16] = jnp.zeros((5, D), F32)

    feat_t = feat.astype(F32).T.astype(BF)
    for j in range(5):
        part = dot_nt(feat_t, slope_s[256 * j : 256 * j + 256])
        for k in range(2):
            base = 256 * (2 * j + k)
            g_ref[base : base + 256] = part[:, 128 * k : 128 * k + 128].astype(BF)
    dfeat = dot_tn(slope_s[...], whead_ref[...])
    scale_f = rms(xf)
    hat = xf * scale_f
    e_ref[8:9] = jnp.sum(dfeat * hat, axis=0, keepdims=True)
    inner = dfeat * gain_f
    dxf = scale_f * (inner - hat * jnp.mean(inner * hat, axis=-1, keepdims=True))
    dx_s[...] = jnp.zeros(dx_s.shape, F32)
    dx_s[:, 1] = dxf.reshape(seqs, STEPS, D)

    for layer in reversed(range(LAYERS)):
        gain_a = small_ref[4 * layer : 4 * layer + 1]
        gain_b = small_ref[4 * layer + 1 : 4 * layer + 2]
        e_ref[4 * layer : 4 * layer + 4] = jnp.zeros((4, D), F32)

        @pl.loop(0, chunks)
        def _(c):
            rows = pl.ds(pl.multiple_of(c * rows_c, rows_c), rows_c)
            dy = dx_s[pl.ds(c * CHUNK, CHUNK)].reshape(rows_c, D)
            dyl = dy.astype(BF)
            dyl_s[rows] = dyl
            for j in range(FF // 256):
                cols = slice(256 * j, 256 * j + 256)
                dact = dot_nt(dyl, wdown_ref[layer, cols])
                gp_s[layer, rows, cols] = (dact * gp_s[layer, rows, cols].astype(F32)).astype(BF)
            dlow = dot_nt(gp_s[layer, rows], wup_ref[layer])
            mid = mid_s[layer, rows]
            scale = rms(mid)
            hat = mid * scale
            dgain = jnp.sum(dlow * hat, axis=0, keepdims=True)
            inner = dlow * gain_b
            dmid = scale * (inner - hat * jnp.mean(inner * hat, axis=-1, keepdims=True)) + dy
            e_ref[4 * layer + 1 : 4 * layer + 2] += dgain
            dml = dmid.astype(BF)
            dml_s[rows] = dml
            do = dot_nt(dml, wsq_ref[layer, 0]).astype(BF).astype(F32)
            do = (do * r_s[layer, rows]).astype(BF)
            mass = do.astype(F32) * o_s[layer, rows]
            mass_hi = mass.astype(BF)
            mass_lo = (mass - mass_hi.astype(F32)).astype(BF)
            delta = dot_nn(mass_hi, sum_hk) + dot_nn(mass_lo, sum_hk)
            qu = att_s[layer, rows, 0:256]
            key = att_s[layer, rows, 512:768]
            val = att_s[layer, rows, 768:1024]
            draws = []
            for b in range(CHUNK):
                span = slice(TOKS * b, TOKS * b + TOKS)
                probs = pu_s[layer, pl.ds(pl.multiple_of(c * rows_c + TOKS * b, TOKS), TOKS)]
                dprob = dot_nt(do[span], expand(val[span]))
                dscore = (probs.astype(F32) * (dprob - delta[span])).astype(BF)
                wide = dscore.astype(F32)
                draws.append(
                    [unskew(wide[STEPS * k : STEPS * k + STEPS]).astype(BF) for k in range(3)]
                )
                dval = fold(dot_tn(probs, do[span])).astype(BF)
                dkey = (fold(dot_tn(dscore, qu[span])) * SCALE).astype(BF)
                l_s[span] = dot_nn(dscore, expand(key[span])) * SCALE
                out_rows = pl.ds(pl.multiple_of(c * rows_c + TOKS * b, TOKS), TOKS)
                pu_s[layer, out_rows] = jnp.concatenate(draws[b], axis=0)
                att_s[layer, out_rows, 512:768] = dkey
                att_s[layer, out_rows, 768:1024] = dval
            dqv = [
                dot_nn(
                    jnp.concatenate([draws[b][k] for b in range(CHUNK)], axis=0), rk_s[layer, k]
                ).reshape(CHUNK, 1, STEPS, D)
                for k in range(3)
            ]
            dqv = jnp.concatenate(dqv, axis=1).reshape(rows_c, D) * SCALE
            dqu = l_s[...]
            e_ref[4 * layer + 2 : 4 * layer + 3] += jnp.sum(dqu, axis=0, keepdims=True)
            e_ref[4 * layer + 3 : 4 * layer + 4] += jnp.sum(dqv, axis=0, keepdims=True)
            dq = (dqu + dqv).astype(BF)
            att_s[layer, rows, 0:256] = dq
            dlow = (
                dot_nt(dq, wqkv_ref[layer, :, :256])
                + dot_nt(att_s[layer, rows, 512:768], wqkv_ref[layer, :, 256:512])
                + dot_nt(att_s[layer, rows, 768:1024], wqkv_ref[layer, :, 512:])
            )
            x = x_s[layer, pl.ds(c * CHUNK, CHUNK)].reshape(rows_c, D)
            scale = rms(x)
            hat = x * scale
            e_ref[4 * layer : 4 * layer + 1] += jnp.sum(dlow * hat, axis=0, keepdims=True)
            inner = dlow * gain_a
            dx = scale * (inner - hat * jnp.mean(inner * hat, axis=-1, keepdims=True)) + dmid
            dx_s[pl.ds(c * CHUNK, CHUNK)] = dx.reshape(CHUNK, 3, STEPS, D)

        base = 2560 + 6656 * (LAYERS - 1 - layer)

        def put(offset, value):
            size = value.shape[0]
            for k in range(2):
                at = base + offset + k * size
                if not isinstance(at, int):
                    at = pl.multiple_of(at, 256)
                g_ref[pl.ds(at, size)] = value[:, 128 * k : 128 * k + 128].astype(BF)

        for j in range(4):
            part = dot_tn(hb_s[layer, :, 256 * j : 256 * j + 256], dyl_s[...])
            for k in range(2):
                g_ref[base + 1024 * k + 256 * j : base + 1024 * k + 256 * j + 256] = part[
                    :, 128 * k : 128 * k + 128
                ].astype(BF)
        for j in range(4):
            put(2048 + 512 * j, dot_tn(b_s[layer], gp_s[layer, :, 256 * j : 256 * j + 256]))
        put(4096, dot_tn(o_s[layer].astype(BF), dml_s[...]))
        drk = []
        draw = pu_s[layer].reshape(seqs, 3, STEPS, HK)
        qv = att_s[layer, :, 256:512].reshape(seqs, 3, STEPS, D)
        for k in range(3):
            wide = dot_tn(
                draw[:, k].reshape(steps_all, HK), qv[:, k].reshape(steps_all, D)
            )
            drk.append(fold(wide) * SCALE)
        put(4608, dot_tn(pos_ref[...], jnp.concatenate(drk, axis=0).astype(BF)))
        put(5120, dot_tn(a_s[layer], att_s[layer, :, 0:256]))
        put(5632, dot_tn(a_s[layer], att_s[layer, :, 512:768]))
        put(6144, dot_tn(a_s[layer], att_s[layer, :, 768:1024]))

    dtok = [dx_s[:, k].reshape(steps_all, D).astype(BF) for k in range(3)]
    base = 2560 + 6656 * LAYERS
    class_row = (iota((256, steps_all), 0) % CLASSES).astype(F32)
    for k in range(2):
        for j in range(2):
            wide = dot_nt(spread_t[256 * j : 256 * j + 256], codes[k].astype(BF))
            hot = (wide == class_row).astype(F32).astype(BF)
            part = dot_nn(hot, dtok[0])
            for h in range(2):
                at = base + 1280 * h + 512 * k + 256 * j
                g_ref[at : at + 256] = part[:, 128 * h : 128 * h + 128].astype(BF)
    row = iota((288, steps_all), 0)
    hot_a = (row == action_row.astype(jnp.int32)).astype(F32).astype(BF)
    hot_r = (row == (reward_row + NA).astype(jnp.int32)).astype(F32).astype(BF)
    part = dot_nn(hot_a, dtok[1]) + dot_nn(hot_r, dtok[2])
    for h in range(2):
        at = base + 1280 * h + 1024
        g_ref[at : at + 256] = part[:256, 128 * h : 128 * h + 128].astype(BF)
    e_ref[16:40] = part[256:280]


def compute(codes, seg, pos, small, table, wqkv, wsq, wup, wdown, whead_t):
    seqs = codes.shape[1]
    toks = seqs * TOKS
    f32, bf = jnp.float32, jnp.bfloat16
    vmem = pltpu.VMEM
    return pl.pallas_call(
        compute_kernel,
        out_shape=(
            jax.ShapeDtypeStruct((2560 + 6656 * LAYERS + 2560, 128), bf),
            jax.ShapeDtypeStruct((40, D), f32),
        ),
        in_specs=[pl.BlockSpec(memory_space=vmem)] * 10,
        out_specs=[pl.BlockSpec(memory_space=vmem)] * 2,
        scratch_shapes=[
            vmem((LAYERS + 1, seqs, 3, STEPS, D), f32),
            vmem((LAYERS, toks, 1024), bf),
            vmem((LAYERS, toks, HK), bf),
            vmem((LAYERS, toks, D), f32),
            vmem((LAYERS, toks, D), f32),
            vmem((LAYERS, toks, D), f32),
            vmem((LAYERS, toks, FF), bf),
            vmem((LAYERS, toks, FF), bf),
            vmem((LAYERS, toks, D), bf),
            vmem((LAYERS, toks, D), bf),
            vmem((toks, D), bf),
            vmem((toks, D), bf),
            vmem((seqs, 3, STEPS, D), f32),
            vmem((LAYERS, 3, HK, D), bf),
            vmem((seqs, STEPS, 128), f32),
            vmem((CHUNK * TOKS, D), f32),
            vmem((HCOLS, seqs * STEPS), bf),
        ],
        compiler_params=pltpu.CompilerParams(vmem_limit_bytes=VMEM_LIMIT),
        name="step",
    )(codes, seg, pos, small, table, wqkv, wsq, wup, wdown, whead_t)


def mesh_bits(streams, groups):
    bits = [("stream", 1)]
    step = 2
    rest = []
    while step < streams:
        rest.append(("stream", step))
        step *= 2
    step, others = 1, []
    while step < groups:
        others.append(("seq", step))
        step *= 2
    return bits, [others[:1], rest, others[1:]]


def bit_orders(streams, groups):
    first, parts = mesh_bits(streams, groups)
    orders = []
    for k in range(3):
        turned = parts[k:] + parts[:k]
        orders.append(first + [b for part in turned for b in part])
    return orders


def ring_plan(total, streams, groups):
    devices = streams * groups
    orders = bit_orders(streams, groups)
    unit = 16 * devices
    subs = 2 if total % (2 * 3 * unit) == 0 else 1
    rows = total // (3 * subs)
    assert rows % unit == 0
    lanes, recv = [], 0
    for sub in range(subs):
        for k in range(3):
            steps, size = [], rows
            for _ in orders[k]:
                size //= 2
                steps.append((size, recv))
                recv += size
            lanes.append(
                dict(base=(3 * sub + k) * rows, rows=rows, order=orders[k], steps=steps, sub=sub)
            )
    return lanes, recv


def place_of(bit):
    axis, step = bit
    return (lax.axis_index(axis) // step) % 2


def partner_of(bit):
    axis, step = bit
    me = lax.axis_index(axis)
    other = me + step * (1 - 2 * ((me // step) % 2))
    if axis == "stream":
        return (other, lax.axis_index("seq"))
    return (lax.axis_index("stream"), other)


class Lane:
    def __init__(self, index, spec, g_ref, out_ref, recv_ref, sems):
        self.spec, self.g, self.out = spec, g_ref, out_ref
        self.recv, self.sems, self.index = recv_ref, sems, index
        offset = spec["base"]
        self.keep, self.send = [], []
        for bit, (size, _) in zip(spec["order"], spec["steps"]):
            mine = place_of(bit)
            self.keep.append(pl.multiple_of(offset + mine * size, 16))
            self.send.append(pl.multiple_of(offset + (1 - mine) * size, 16))
            offset = self.keep[-1]

    def scatter(self, i):
        size, slot = self.spec["steps"][i]
        return pltpu.make_async_remote_copy(
            src_ref=self.g.at[pl.ds(self.send[i], size)],
            dst_ref=self.recv.at[pl.ds(slot, size)],
            send_sem=self.sems.at[0, self.index, i],
            recv_sem=self.sems.at[1, self.index, i],
            device_id=partner_of(self.spec["order"][i]),
            device_id_type=pl.DeviceIdType.MESH,
        )

    def gather(self, i):
        size, _ = self.spec["steps"][i]
        rows = pl.ds(self.keep[i], size)
        return pltpu.make_async_remote_copy(
            src_ref=self.out.at[rows],
            dst_ref=self.out.at[rows],
            send_sem=self.sems.at[2, self.index, i],
            recv_sem=self.sems.at[3, self.index, i],
            device_id=partner_of(self.spec["order"][i]),
            device_id_type=pl.DeviceIdType.MESH,
        )

    def add(self, i):
        size, slot = self.spec["steps"][i]
        target = self.out if i + 1 == len(self.keep) else self.g
        block = 96
        while size % block:
            block //= 2

        @pl.loop(0, size // block)
        def _(j):
            at = pl.ds(pl.multiple_of(self.keep[i] + j * block, 16), block)
            got = pl.ds(pl.multiple_of(slot + j * block, 16), block)
            target[at] = (self.g[at].astype(F32) + self.recv[got].astype(F32)).astype(BF)


def reduce_kernel(streams, groups, g_ref, e_ref, go_ref, eo_ref, work_s, recv_s, slot_s, got_s, sems, esems, lsem):
    lanes, _ = ring_plan(g_ref.shape[0], streams, groups)
    order = lanes[0]["order"]
    rounds = len(order)
    load = pltpu.make_async_copy(g_ref, work_s, lsem)
    load.start()
    barrier = pltpu.get_barrier_semaphore()
    for bit in order:
        pl.semaphore_signal(
            barrier, inc=1, device_id=partner_of(bit), device_id_type=pl.DeviceIdType.MESH
        )
    slot_s[0] = e_ref[...]
    pl.semaphore_wait(barrier, rounds)
    load.wait()

    def extra(i):
        return pltpu.make_async_remote_copy(
            src_ref=slot_s.at[i],
            dst_ref=got_s.at[i],
            send_sem=esems.at[0, i],
            recv_sem=esems.at[1, i],
            device_id=partner_of(order[i]),
            device_id_type=pl.DeviceIdType.MESH,
        )

    runs = [Lane(n, spec, work_s, go_ref, recv_s, sems) for n, spec in enumerate(lanes)]
    extra(0).start()
    for run in runs:
        run.scatter(0).start()
    for i in range(rounds):
        extra(i).wait()
        slot_s[i + 1] = slot_s[i] + got_s[i]
        if i + 1 < rounds:
            extra(i + 1).start()
        for run in runs:
            run.scatter(i).wait()
            run.add(i)
            if i + 1 < rounds:
                run.scatter(i + 1).start()
            else:
                run.gather(i).start()
    eo_ref[...] = slot_s[rounds]
    for i in reversed(range(rounds)):
        for run in runs:
            run.gather(i).wait()
            if i:
                run.gather(i - 1).start()


def reduce_all(grads, extra, streams, groups):
    lanes, recv = ring_plan(grads.shape[0], streams, groups)
    rounds = len(lanes[0]["order"])
    vmem = pltpu.VMEM
    return pl.pallas_call(
        lambda *refs: reduce_kernel(streams, groups, *refs),
        out_shape=(
            jax.ShapeDtypeStruct(grads.shape, grads.dtype),
            jax.ShapeDtypeStruct(extra.shape, extra.dtype),
        ),
        in_specs=[pl.BlockSpec(memory_space=pl.ANY), pl.BlockSpec(memory_space=vmem)],
        out_specs=[pl.BlockSpec(memory_space=vmem)] * 2,
        scratch_shapes=[
            vmem(grads.shape, BF),
            vmem((recv, 128), BF),
            vmem((rounds + 1,) + extra.shape, F32),
            vmem((rounds,) + extra.shape, F32),
            pltpu.SemaphoreType.DMA((4, len(lanes), rounds)),
            pltpu.SemaphoreType.DMA((2, rounds)),
            pltpu.SemaphoreType.DMA,
        ],
        compiler_params=pltpu.CompilerParams(
            collective_id=0, has_side_effects=True, vmem_limit_bytes=24 * 1000 * 1000
        ),
        name="reduce",
    )(grads, extra)


def update_pieces():
    pieces = []
    for k in range(LAYERS):
        layer = LAYERS - 1 - k
        base = 2560 + 6656 * k
        for half in range(2):
            r = 512 * half
            pieces.append(
                (4, (layer,), r, 512, [(base + 1024 * j + r, 128 * j) for j in range(2)])
            )
        pieces.append((3, (layer,), 0, 256, [(base + 2048 + 256 * j, 128 * j) for j in range(8)]))
        pieces.append((2, (layer, 0), 0, 256, [(base + 4096 + 256 * j, 128 * j) for j in range(2)]))
        pieces.append((2, (layer, 1), 0, 256, [(base + 4608 + 256 * j, 128 * j) for j in range(2)]))
        pieces.append((1, (layer,), 0, 256, [(base + 5120 + 256 * j, 128 * j) for j in range(6)]))
    pieces.append((6, (), 0, 256, [(256 * j, 128 * j) for j in range(10)]))
    base = 2560 + 6656 * LAYERS
    pieces.append((0, (), 0, 1280, [(base + 1280 * j, 128 * j) for j in range(2)]))
    return pieces


def update_kernel(clip_value, step_rate, *refs):
    g_ref, e_ref = refs[:2]
    ins = refs[2:23]
    stat_ref = refs[23]
    outs = refs[24:45]
    bufs = refs[45:66]
    isem, osem = refs[66:]
    pieces = update_pieces()
    table_rows = ins[0].shape[0]
    tail = table_rows - 1280

    def view(ref, piece):
        array, lead, first, rows, _ = piece
        if lead:
            ref = ref.at[lead]
        if ref.shape[0] == rows:
            return ref
        return ref.at[pl.ds(first, rows)]

    def transfer(kind, n, k, piece):
        src, dst = (ins, bufs) if kind == 0 else (bufs, outs)
        array = piece[0]
        sem = (isem, osem)[kind].at[k, n]
        return pltpu.make_async_copy(
            view(src[7 * k + array], piece), view(dst[7 * k + array], piece), sem
        )

    specials = [(0, (), 1280, tail, None), (5, (), 0, ins[5].shape[0], None)]
    order = specials + pieces
    for n, piece in enumerate(order):
        for k in range(3):
            transfer(0, n, k, piece).start()

    block = 128
    count = g_ref.shape[0] // block

    def gather(j, total):
        v = g_ref[pl.ds(pl.multiple_of(j * block, block), block)].astype(F32)
        return total + jnp.sum((v * v).reshape(block // 8, 8, 128), axis=0)

    total = lax.fori_loop(0, count, gather, jnp.zeros((8, 128), F32))
    rest = jnp.sum(e_ref[0:9] * e_ref[0:9]) + jnp.sum(e_ref[16:40] * e_ref[16:40])
    loss = jnp.max(e_ref[9:10])
    terms = jnp.max(e_ref[10:11])
    inverse = 1.0 / jnp.full((8, 128), terms, F32)
    norm = jnp.sqrt(jnp.full((8, 128), jnp.sum(total) + rest, F32)) * inverse
    factor = inverse * clip_value / jnp.maximum(norm, clip_value)
    stat_ref[0:8] = jnp.full((8, 128), loss, F32)
    stat_ref[8:16] = jnp.full((8, 128), terms, F32)
    stat_ref[16:24] = norm
    factor = factor[:1]

    def advance(views, rows, cols, gradient, scale):
        w, m, e = [v[rows, cols] for v in views]
        clipped = gradient * scale
        moment = MOMENTUM_RATE * m + clipped
        weight = w - step_rate * (clipped + MOMENTUM_RATE * moment)
        views[0][rows, cols] = weight
        views[1][rows, cols] = moment
        views[2][rows, cols] = AVERAGE_RATE * e + (1.0 - AVERAGE_RATE) * weight

    for n, piece in enumerate(order):
        array, lead, first, rows, blocks = piece
        for k in range(3):
            transfer(0, n, k, piece).wait()
        views = [bufs[7 * k + array].at[lead] if lead else bufs[7 * k + array] for k in range(3)]
        if blocks is None:
            at = 16 if array == 0 else 0
            wide = jnp.concatenate([factor, factor], axis=1)
            advance(
                views, slice(first, first + rows), slice(0, D), e_ref[at : at + rows], wide
            )
        else:
            step = 64

            @pl.loop(0, rows // step)
            def _(j):
                for source, column in blocks:
                    g = g_ref[pl.ds(pl.multiple_of(source + j * step, step), step)].astype(F32)
                    at = pl.ds(pl.multiple_of(first + j * step, step), step)
                    advance(views, at, slice(column, column + 128), g, factor)

        for k in range(3):
            transfer(1, n, k, piece).start()
    for n, piece in enumerate(order):
        for k in range(3):
            transfer(1, n, k, piece).wait()


def update_all(grads, extra, arrays, clip_value, step_rate):
    vmem = pltpu.VMEM
    count = len(update_pieces()) + 2
    hbm = pl.BlockSpec(memory_space=pl.ANY)
    results = pl.pallas_call(
        lambda *refs: update_kernel(clip_value, step_rate, *refs),
        out_shape=[jax.ShapeDtypeStruct((24, 128), F32)]
        + [jax.ShapeDtypeStruct(a.shape, F32) for a in arrays],
        in_specs=[pl.BlockSpec(memory_space=vmem)] * 2 + [hbm] * 21,
        out_specs=[pl.BlockSpec(memory_space=vmem)] + [hbm] * 21,
        scratch_shapes=[vmem(a.shape, F32) for a in arrays]
        + [pltpu.SemaphoreType.DMA((3, count)), pltpu.SemaphoreType.DMA((3, count))],
        compiler_params=pltpu.CompilerParams(vmem_limit_bytes=44 * 1000 * 1000),
        name="update",
    )(grads, extra, *arrays)
    return results[0], results[1:]


def on_device(step_codes, segments, *arrays):
    stream_id = lax.axis_index("stream")
    streams = lax.axis_size("stream")
    groups = lax.axis_size("seq")
    group_seqs = step_codes.shape[0]
    own = group_seqs // streams
    codes = lax.all_to_all(
        step_codes.reshape(streams, own, STEPS, -1), "stream", split_axis=0, concat_axis=0
    )
    seg = lax.dynamic_slice_in_dim(segments, stream_id * own, own, 0)
    table, qkv, square, up, down, small, head = arrays[:7]
    table_low = jnp.pad(table.astype(BF), ((0, TROWS - table.shape[0]), (0, 0)))
    pos = jnp.asarray(position_rows()).astype(BF)
    grads, extra = compute(
        codes,
        seg,
        pos,
        small,
        table_low,
        qkv.astype(BF),
        square.astype(BF),
        up.astype(BF),
        down.astype(BF),
        head.astype(BF).T,
    )
    grads, extra = reduce_all(grads, extra, streams, groups)
    params_total = sum(w.size for w in arrays[:7])
    clip_value = CLIP_SCALE * (group_seqs * groups * STEPS) ** (-0.5)
    step_rate = STEP_SCALE * params_total**0.5 / clip_value
    stats, updated = update_all(grads, extra, arrays, clip_value, step_rate)
    return (stats[0, 0], stats[8, 0], stats[16, 0], *updated)


def solution(mesh):
    return jax.shard_map(
        on_device,
        mesh=mesh,
        in_specs=(P("seq", None, "stream"), P("seq", None)) + (P(),) * 21,
        out_specs=(P(),) * 24,
        check_vma=False,
    )
```

profile of v0, /device:TPU:0, one launch (start us, length us, event | category | flops | bytes accessed | tf_op | source)
XLA Modules:
  0.0 206.3 jit_solution(6950916045696938970)
XLA Ops:
  0.7 1.2 reshape.51
  1.9 0.9 reshape.52
  2.8 4.2 %all-to-all-start = ((s32[4,1,8192]{2,1,0:T(1,128)}), s32[4,1,8192]{2,1,0:T(1,128)S(1)}, u32[]{:S(2)}, u32[]{:S(2)}) async-start(s32[4,1,8192]{2,1,0:T(1,128)} %reshape.52), calls=%async_computation | async-start | bytes 262144 | tf_op jit(solution)/shard_map/all_to_all | solution.py:844
  7.8 2.2 %convert_element_type.26.wsq_ref = bf16[2,2,256,256]{3,2,1,0:T(8,128)(2,1)} convert(f32[2,2,256,256]{3,2,1,0:T(8,128)} %refs_4_.1) | non-fusion elementwise | flops 262144 | bytes 1572864 | tf_op jit(solution)/shard_map/convert_element_type | solution.py:858
  10.0 1.1 copy.56
  11.1 1.3 copy-done.19
  12.5 1.0 convert_element_type.25.wqkv_ref
  13.4 0.9 copy-done.17
  14.4 1.1 convert_element_type.27.wup_ref
  15.5 0.8 copy-done.18
  16.3 1.1 convert_element_type.28.wdown_ref
  17.4 0.9 pad.4.table_ref
  18.8 1.0 reduce.1
  20.0 1.4 copy.57.codes_ref
  21.4 95.3 %step.1 = (bf16[18432,128]{1,0:T(8,128)(2,1)}, f32[40,256]{1,0:T(8,128)}) custom-call(s32[4,32,16,16]{3,2,1,0:T(8,128)} %copy.57.codes_ref, s32[32,16]{1,0:T(8,128)} %copy.58.seg_ref, bf16[144,256]{1,0:T(8,128)(2,1)} %constant.18.pos_ref, f32[9,256]{1,0:T(8,128)} %refs_7_.1, bf16[1408,256]{1,0:T(8,128)(2,1)} %pad.4.table_ref, ...), custom_call_target="tpu_custom_call" | custom-call | tf_op jit(solution)/shard_map/step/pallas_call | solution.py:495
  116.6 2.3 %copy-done.5 = bf16[18432,128]{1,0:T(8,128)(2,1)S(1)} copy-done((bf16[18432,128]{1,0:T(8,128)(2,1)S(1)}, bf16[18432,128]{1,0:T(8,128)(2,1)}, u32[]{:S(2)}) %copy-start.5) | copy-done | bytes 4718616
  119.0 0.8 copy-done.14
  119.8 61.5 %reduce.2 = (bf16[18432,128]{1,0:T(8,128)(2,1)S(1)}, f32[40,256]{1,0:T(8,128)S(1)}) custom-call(bf16[18432,128]{1,0:T(8,128)(2,1)S(1)} %copy-done.5, f32[40,256]{1,0:T(8,128)S(1)} %copy-done.14), custom_call_target="tpu_custom_call" | custom-call | tf_op jit(solution)/shard_map/reduce/pallas_call | solution.py:687
  181.3 2.1 %copy-done.4 = bf16[18432,128]{1,0:T(8,128)(2,1)} copy-done((bf16[18432,128]{1,0:T(8,128)(2,1)}, bf16[18432,128]{1,0:T(8,128)(2,1)S(1)}, u32[]{:S(2)}) %copy-start.4) | copy-done | bytes 4718616
  183.5 1.3 copy-done.9
  184.8 1.3 copy-done.10
  186.1 1.2 copy-done.11
  187.4 1.2 copy-done.12
  188.6 17.2 %update.1 = (f32[24,128]{1,0:T(8,128)S(1)}, f32[1297,256]{1,0:T(8,128)}, f32[2,256,768]{2,1,0:T(8,128)}, f32[2,2,256,256]{3,2,1,0:T(8,128)}, f32[2,256,1024]{2,1...) custom-call(bf16[18432,128]{1,0:T(8,128)(2,1)} %copy-done.4, ...), custom_call_target="tpu_custom_call" | custom-call | tf_op jit(solution)/shard_map/update/pallas_call | solution.py:824
  (38 shorter events, 2.1 us)
Async XLA Ops:
  0.7 6.4 %copy-start = (s32[128,16]{0,1:T(8,128)S(1)}, s32[128,16]{0,1:T(8,128)}, u32[]{:S(2)}) copy-start(s32[128,16]{0,1:T(8,128)} %param.25) | copy-start | bytes 24580
  1.9 8.1 %copy-start.3 = (f32[256,1280]{1,0:T(8,128)S(1)}, f32[256,1280]{1,0:T(8,128)}, u32[]{:S(2)}) copy-start(f32[256,1280]{1,0:T(8,128)} %refs_8_.1) | copy-start | bytes 3932164
  2.8 15.5 %all-to-all-start = ((s32[4,1,8192]{2,1,0:T(1,128)}), s32[4,1,8192]{2,1,0:T(1,128)S(1)}, u32[]{:S(2)}, u32[]{:S(2)}) async-start(s32[4,1,8192]{2,1,0:T(1,128)} %reshape.52), calls=%async_computation | async-start | bytes 262144 | tf_op jit(solution)/shard_map/all_to_all | solution.py:844
  7.8 3.3 %copy-start.2 = (f32[1297,256]{1,0:T(8,128)S(1)}, f32[1297,256]{1,0:T(8,128)}, u32[]{:S(2)}) copy-start(f32[1297,256]{1,0:T(8,128)} %refs_2_.1) | copy-start | bytes 3984388
  11.1 1.4 copy-start.19
  12.5 1.9 copy-start.17
  14.4 2.0 copy-start.18
  116.6 2.3 %copy-start.5 = (bf16[18432,128]{1,0:T(8,128)(2,1)S(1)}, bf16[18432,128]{1,0:T(8,128)(2,1)}, u32[]{:S(2)}) copy-start(bf16[18432,128]{1,0:T(8,128)(2,1)} %get-tuple-element.50.refs_0_) | copy-start | bytes 14155780
  119.0 0.8 copy-start.14
  119.8 63.7 %copy-start.6 = (f32[2,2,256,256]{3,2,1,0:T(8,128)S(1)}, f32[2,2,256,256]{3,2,1,0:T(8,128)}, u32[]{:S(2)}) copy-start(f32[2,2,256,256]{3,2,1,0:T(8,128)} %refs_4_.1) | copy-start | bytes 3145732
  119.8 63.7 %copy-start.7 = (f32[1297,256]{1,0:T(8,128)S(1)}, f32[1297,256]{1,0:T(8,128)}, u32[]{:S(2)}) copy-start(f32[1297,256]{1,0:T(8,128)} %refs_9_.1) | copy-start | bytes 3984388
  119.8 63.7 %copy-start.8 = (f32[1297,256]{1,0:T(8,128)S(1)}, f32[1297,256]{1,0:T(8,128)}, u32[]{:S(2)}) copy-start(f32[1297,256]{1,0:T(8,128)} %refs_16_.1) | copy-start | bytes 3984388
  119.8 63.7 %copy-start.13 = (f32[9,256]{1,0:T(8,128)S(1)}, f32[9,256]{1,0:T(8,128)}, u32[]{:S(2)}) copy-start(f32[9,256]{1,0:T(8,128)} %refs_7_.1) | copy-start | bytes 27652
  119.8 63.7 %copy-start.15 = (f32[9,256]{1,0:T(8,128)S(1)}, f32[9,256]{1,0:T(8,128)}, u32[]{:S(2)}) copy-start(f32[9,256]{1,0:T(8,128)} %refs_14_.1) | copy-start | bytes 27652
  119.8 63.7 %copy-start.16 = (f32[9,256]{1,0:T(8,128)S(1)}, f32[9,256]{1,0:T(8,128)}, u32[]{:S(2)}) copy-start(f32[9,256]{1,0:T(8,128)} %refs_21_.1) | copy-start | bytes 27652
  181.3 2.1 %copy-start.4 = (bf16[18432,128]{1,0:T(8,128)(2,1)}, bf16[18432,128]{1,0:T(8,128)(2,1)S(1)}, u32[]{:S(2)}) copy-start(bf16[18432,128]{1,0:T(8,128)(2,1)S(1)} %get-tuple-element.52.refs_0_) | copy-start | bytes 14155780
  183.5 1.3 copy-start.9
  184.8 1.3 copy-start.10
  186.1 1.2 copy-start.11
  187.4 1.2 copy-start.12
  188.6 17.7 %copy-start.1 = (s32[128,16]{0,1:T(8,128)S(1)}, s32[128,16]{0,1:T(8,128)}, u32[]{:S(2)}) copy-start(s32[128,16]{0,1:T(8,128)} %param.25) | copy-start | bytes 24580
where the time goes:
time: 207 us; the launch traced here: 206 us
  Pallas kernels  174 us (84%)
  local copies, waits for them, and re-layouts  20.9 us (10%)
  other arithmetic  6.37 us (3%)
  starting transfers between devices  4.24 us (2%)
    pallas_call x1, Pallas kernels, compute(): pl.pallas_call(compute_kernel, out_shape=(jax.ShapeDtypeStruct((2560 + 66...  95.3 us
    pallas_call x1, Pallas kernels, reduce_all(): pl.pallas_call(lambda *refs: reduce_kernel(streams, groups, *refs), out_s...  61.5 us
    pallas_call x1, Pallas kernels, update_all(): pl.pallas_call(lambda *refs: update_kernel(clip_value, step_rate, *refs),...  17.2 us
    unnamed x44, local copies, waits for them, and re-layouts  16.3 us
    all_to_all x1, starting transfers between devices, on_device(): lax.all_to_all(step_codes.reshape(streams, own, STEPS, -1), 'stream', spl...  4.24 us
  transfers between devices with their start and end apart: 1, of which 0 were waited for; matrix products, arithmetic and copies ran while one was open for 4% of the time, Pallas kernels for 0%

commit v1 on v0

v1 whole, which is shorter than its diff:
```python
import math

import jax
import jax.numpy as jnp
import numpy as np
from jax import lax
from jax.experimental import pallas as pl
from jax.experimental.pallas import tpu as pltpu
from jax.sharding import PartitionSpec as P

D = 256
HEADS = 8
HD = 32
FF = 1024
CATS = 32
CLASSES = 32
NA = 18
STEPS = 16
TOKS = 48
HK = HEADS * TOKS
LAYERS = 2
HCOLS = 1280
TROWS = 1408
CHUNK = 8
EPSILON = 1e-06
MOMENTUM_RATE = 0.9
AVERAGE_RATE = 0.7
CLIP_SCALE = 0.2
STEP_SCALE = 0.03
MASKED = -1e30
POSITION_SCALE = 0.5
SCALE = HD ** (-0.5)
BF = jnp.bfloat16
F32 = jnp.float32
VMEM_LIMIT = 63 * 1000 * 1000


def dot_nn(a, b):
    return lax.dot_general(a, b, (((1,), (0,)), ((), ())), preferred_element_type=F32)


def dot_nt(a, b):
    return lax.dot_general(a, b, (((1,), (1,)), ((), ())), preferred_element_type=F32)


def dot_tn(a, b):
    return lax.dot_general(a, b, (((0,), (0,)), ((), ())), preferred_element_type=F32)


def iota(shape, dim):
    return lax.broadcasted_iota(jnp.int32, shape, dim)


def position_rows():
    distance = np.arange(TOKS, dtype=np.float32)[:, None]
    rates = np.exp(np.arange(D // 2, dtype=np.float32) * np.float32(-2.0 * math.log(10000.0) / D))
    angle = (distance * rates[None, :].astype(np.float32)).astype(np.float32)
    table = np.float32(POSITION_SCALE) * np.concatenate([np.sin(angle), np.cos(angle)], axis=1)
    rows = np.zeros((3, TOKS, D), np.float32)
    for i in range(3):
        for j in range(3):
            for e in range(STEPS):
                d = 3 * (STEPS - 1 - e) + i - j
                if d >= 0:
                    rows[i, j * STEPS + e] = table[d]
    return rows.reshape(3 * TOKS, D)


def rms(values):
    return lax.rsqrt(jnp.mean(values * values, axis=-1, keepdims=True) + EPSILON)


def head_mask(h, rows):
    lane = iota((rows, 128), 1)
    low = (h % 4) * HD
    return ((lane >= low) & (lane < low + HD)).astype(F32).astype(BF)


def expand(rows):
    zero = jnp.zeros((TOKS, 128), BF)
    parts = []
    for h in range(HEADS):
        half = rows[:, 128 * (h // 4) : 128 * (h // 4) + 128] * head_mask(h, TOKS)
        parts.append(jnp.concatenate([half, zero] if h < 4 else [zero, half], axis=1))
    return jnp.concatenate(parts, axis=0)


def fold(values):
    lane = iota((TOKS, 128), 1)
    halves = []
    for g in range(2):
        total = None
        for h in range(4):
            part = values[(4 * g + h) * TOKS : (4 * g + h + 1) * TOKS, 128 * g : 128 * g + 128]
            total = part if total is None else jnp.where(lane >= h * HD, part, total)
        halves.append(total)
    return jnp.concatenate(halves, axis=1)


def spans(tile):
    found = []
    for h in range(HEADS):
        low, high = max(TOKS * h - 128 * tile, 0), min(TOKS * (h + 1) - 128 * tile, 128)
        if low < high:
            found.append((h, low, high))
    return found


def segment_max(scores):
    rows = scores.shape[0]
    lane = iota((rows, 128), 1)
    tiles = [scores[:, 128 * t : 128 * t + 128] for t in range(3)]
    best = {}
    for t in range(3):
        for h, low, high in spans(t):
            part = jnp.where((lane >= low) & (lane < high), tiles[t], -3e38)
            best[h] = part if h not in best else jnp.maximum(best[h], part)
    best = {h: jnp.max(v, axis=1, keepdims=True) for h, v in best.items()}
    outs = []
    for t in range(3):
        total = None
        for h, low, high in spans(t):
            wide = jnp.broadcast_to(best[h], (rows, 128))
            total = wide if total is None else jnp.where(lane >= low, wide, total)
        outs.append(total)
    return jnp.concatenate(outs, axis=1)


def unskew(values):
    row = iota((STEPS, HK), 0)
    values = jnp.concatenate(
        [pltpu.roll(values[:8], 15, 1), pltpu.roll(values[8:], 7, 1)], axis=0
    )
    for bit in (1, 2, 4):
        values = jnp.where((row & bit) > 0, pltpu.roll(values, HK - bit, 1), values)
    return values


SECTIONS = (2560, 4096, 2560, 4096, 5120)


def bit_orders(streams, groups):
    first, rest, others = [("stream", 1)], [], []
    step = 2
    while step < streams:
        rest.append(("stream", step))
        step *= 2
    step = 1
    while step < groups:
        others.append(("seq", step))
        step *= 2
    near, far = others[:1], others[1:]
    return [first + near + rest + far, first + rest + near + far, first + far + near + rest]


def exchange_plan(streams, groups):
    unit = 16 * streams * groups
    sections = SECTIONS
    if any(s % unit or s < 3 * unit for s in sections):
        sections = (sum(SECTIONS),)
    orders = bit_orders(streams, groups)
    plan, base, recv, own = [], 0, 0, 0
    for rows in sections:
        units = rows // unit
        last = max(1, round(0.222 * units))
        parts = [(units - last + 1) // 2, (units - last) // 2, last]
        lanes = []
        for part, order in zip(parts, orders):
            size, steps = part * unit, []
            for _ in order:
                size //= 2
                steps.append((size, recv))
                recv += size
            lanes.append(dict(base=base, order=order, steps=steps, own=own))
            own += size
            base += part * unit
        plan.append(lanes)
    assert base == sum(SECTIONS)
    return plan, recv, own


def place_of(bit):
    axis, step = bit
    return (lax.axis_index(axis) // step) % 2


def partner_of(bit):
    axis, step = bit
    me = lax.axis_index(axis)
    other = me + step * (1 - 2 * ((me // step) % 2))
    if axis == "stream":
        return (other, lax.axis_index("seq"))
    return (lax.axis_index("stream"), other)


class Lane:
    def __init__(self, spec, refs, sems, own_sem):
        self.spec, self.sems, self.own_sem = spec, sems, own_sem
        self.g, self.out, self.recv, self.own = refs
        offset = spec["base"]
        self.keep, self.send = [], []
        for bit, (size, _) in zip(spec["order"], spec["steps"]):
            mine = place_of(bit)
            self.keep.append(pl.multiple_of(offset + mine * size, 16))
            self.send.append(pl.multiple_of(offset + (1 - mine) * size, 16))
            offset = self.keep[-1]

    def remote(self, kind, i, src, dst):
        return pltpu.make_async_remote_copy(
            src_ref=src,
            dst_ref=dst,
            send_sem=self.sems.at[2 * kind, i],
            recv_sem=self.sems.at[2 * kind + 1, i],
            device_id=partner_of(self.spec["order"][i]),
            device_id_type=pl.DeviceIdType.MESH,
        )

    def scatter(self, i):
        size, slot = self.spec["steps"][i]
        return self.remote(
            0, i, self.g.at[pl.ds(self.send[i], size)], self.recv.at[pl.ds(slot, size)]
        )

    def mine(self):
        return self.own.at[pl.ds(self.spec["own"], self.spec["steps"][-1][0])]

    def keep_copy(self):
        rows = pl.ds(self.keep[-1], self.spec["steps"][-1][0])
        return pltpu.make_async_copy(self.mine(), self.out.at[rows], self.own_sem)

    def gather(self, i):
        size, _ = self.spec["steps"][i]
        rows = pl.ds(self.keep[i], size)
        last = i + 1 == len(self.keep)
        return self.remote(1, i, self.mine() if last else self.out.at[rows], self.out.at[rows])

    def add(self, i):
        size, slot = self.spec["steps"][i]
        last = i + 1 == len(self.keep)
        block = 128
        while size % block:
            block //= 2

        @pl.loop(0, size // block)
        def _(j):
            at = pl.ds(pl.multiple_of(self.keep[i] + j * block, 16), block)
            got = pl.ds(pl.multiple_of(slot + j * block, 16), block)
            value = (self.g[at].astype(F32) + self.recv[got].astype(F32)).astype(BF)
            if last:
                own = pl.multiple_of(self.spec["own"] + j * block, 16)
                self.own[pl.ds(own, block)] = value
            else:
                self.g[at] = value


class Exchange:
    def __init__(self, streams, groups, g_ref, out_ref, recv_ref, own_ref, sems, own_sems):
        plan, _, _ = exchange_plan(streams, groups)
        refs = (g_ref, out_ref, recv_ref, own_ref)
        self.sections = [
            [
                Lane(spec, refs, sems.at[n, k], own_sems.at[n, k])
                for k, spec in enumerate(lanes)
            ]
            for n, lanes in enumerate(plan)
        ]
        self.order = plan[0][0]["order"]
        self.rounds = len(self.order)
        self.active = []

    def open(self, n):
        if len(self.sections) > 1:
            for lane in self.sections[n]:
                lane.scatter(0).start()
            self.active.append([n, 0])

    def advance(self, n, stage):
        rounds = self.rounds
        for lane in self.sections[n]:
            if stage < rounds:
                lane.scatter(stage).wait()
                lane.add(stage)
                if stage + 1 < rounds:
                    lane.scatter(stage + 1).start()
                else:
                    lane.keep_copy().start()
                    lane.gather(stage).start()
            else:
                i = 2 * rounds - 1 - stage
                lane.gather(i).wait()
                if i + 1 == rounds:
                    lane.keep_copy().wait()
                if i:
                    lane.gather(i - 1).start()

    def tick(self):
        for item in self.active:
            self.advance(*item)
            item[1] += 1
        self.active = [item for item in self.active if item[1] < 2 * self.rounds]

    def ticks(self, c, count):
        for k in range(count):
            if self.active:
                pl.when(c == k)(self.tick)

    def finish(self, slot_ref, got_ref, sems, total_ref):
        last = len(self.sections) - 1

        def extra(i):
            return pltpu.make_async_remote_copy(
                src_ref=slot_ref.at[i],
                dst_ref=got_ref.at[i],
                send_sem=sems.at[0, i],
                recv_sem=sems.at[1, i],
                device_id=partner_of(self.order[i]),
                device_id_type=pl.DeviceIdType.MESH,
            )

        for lane in self.sections[last]:
            lane.scatter(0).start()
        extra(0).start()
        self.active.append([last, 0])
        i = 0
        while self.active or i < self.rounds:
            if i < self.rounds:
                extra(i).wait()
                slot_ref[i + 1] = slot_ref[i] + got_ref[i]
                if i + 1 < self.rounds:
                    extra(i + 1).start()
            self.tick()
            i += 1
        total_ref[...] = slot_ref[self.rounds]

def step_kernel(
    streams,
    groups,
    codes_hbm,
    seg_ref,
    pos_ref,
    small_ref,
    table_hbm,
    qkv_hbm,
    square_hbm,
    up_hbm,
    down_hbm,
    head_hbm,
    out_hbm,
    total_ref,
    x_s,
    att_s,
    pu_s,
    o_s,
    mid_s,
    hb_s,
    gp_s,
    a_s,
    b_s,
    dyl_s,
    dml_s,
    rk_s,
    start_s,
    l_s,
    slope_s,
    table_s,
    wqkv_s,
    wsq_s,
    wup_s,
    wdown_s,
    whead_s,
    wheadt_s,
    stage_s,
    raw_s,
    send_s,
    codes_s,
    g_s,
    recv_s,
    own_s,
    slot_s,
    got_s,
    load_sems,
    code_sems,
    sems,
    own_sems,
    extra_sems,
):
    toks = x_s.shape[1]
    seqs = toks // TOKS
    steps_all = seqs * STEPS
    chunks = seqs // CHUNK
    rows_c = CHUNK * TOKS
    me = lax.axis_index("stream")
    table_rows = table_hbm.shape[0]

    raw_load = pltpu.make_async_copy(codes_hbm, raw_s, load_sems.at[0])
    raw_load.start()
    loads = [(pltpu.make_async_copy(table_hbm, stage_s, load_sems.at[1]), None, None)]

    def load(src, place, targets):
        copy = pltpu.make_async_copy(src, place, load_sems.at[len(loads) + 1])
        loads.append((copy, place, targets))

    for layer in range(LAYERS):
        places = [o_s.at[layer, pl.ds(256 * j, 256)] for j in range(6)]
        places += [mid_s.at[layer, pl.ds(256 * j, 256)] for j in range(6)]
        places += [x_s.at[1, pl.ds(256 * layer, 256)]]
        places = iter(places)
        for j in range(3):
            cols = pl.ds(256 * j, 256)
            load(qkv_hbm.at[layer, :, cols], next(places), [(wqkv_s.at[layer, :, cols], False)])
        for j in range(2):
            load(square_hbm.at[layer, j], next(places), [(wsq_s.at[layer, j], False)])
        for j in range(4):
            cols = pl.ds(256 * j, 256)
            load(up_hbm.at[layer, :, cols], next(places), [(wup_s.at[layer, :, cols], False)])
        for j in range(4):
            cols = pl.ds(256 * j, 256)
            load(down_hbm.at[layer, cols], next(places), [(wdown_s.at[layer, cols], False)])
    for j in range(HCOLS // 256):
        cols = pl.ds(256 * j, 256)
        load(
            head_hbm.at[:, cols],
            x_s.at[2, cols],
            [(whead_s.at[:, cols], False), (wheadt_s.at[cols], True)],
        )
    for copy, _, _ in loads:
        copy.start()

    comm = Exchange(streams, groups, g_s, out_hbm, recv_s, own_s, sems, own_sems)
    barrier = pltpu.get_barrier_semaphore()
    peers = [((me + j) % streams, lax.axis_index("seq")) for j in range(1, streams)]
    greeted = peers + [partner_of(bit) for bit in comm.order if bit[0] == "seq"]
    for peer in greeted:
        pl.semaphore_signal(
            barrier, inc=1, device_id=peer, device_id_type=pl.DeviceIdType.MESH
        )

    raw_load.wait()
    eye = (iota((STEPS, STEPS), 0) == iota((STEPS, STEPS), 1)).astype(F32).astype(BF)
    for k in range(streams):
        part = raw_s[seqs * k : seqs * k + seqs].reshape(steps_all, STEPS).astype(F32).astype(BF)
        send_s[k] = dot_nt(eye, part).astype(BF)
    pl.semaphore_wait(barrier, len(greeted))
    sends = []
    for j, peer in enumerate(peers):
        sends.append(
            pltpu.make_async_remote_copy(
                src_ref=send_s.at[peer[0]],
                dst_ref=codes_s.at[me],
                send_sem=code_sems.at[0, j],
                recv_sem=code_sems.at[1, j],
                device_id=peer,
                device_id_type=pl.DeviceIdType.MESH,
            )
        )
        sends[-1].start()
    codes_s[me] = send_s[me]

    seg = seg_ref[pl.ds(pl.multiple_of(me * seqs, 8), seqs)].astype(F32)
    seg3 = jnp.broadcast_to(seg[:, None, :], (seqs, STEPS, STEPS))
    i1, i2 = iota((seqs, STEPS, STEPS), 1), iota((seqs, STEPS, STEPS), 2)
    seg_col = jnp.sum(jnp.where(i1 == i2, seg3, 0.0), axis=2, keepdims=True)
    start = jnp.sum(jnp.where(seg3 < seg_col, 1.0, 0.0), axis=2, keepdims=True)
    start_s[...] = jnp.broadcast_to(start, (seqs, STEPS, 128))
    follow = jnp.where((i2 == i1 + 1) & (seg3 == seg_col), 1.0, 0.0).reshape(steps_all, STEPS)
    valid_row = dot_nt(jnp.ones((STEPS, STEPS), BF), follow.astype(BF))[:1]

    loads[0][0].wait()
    whole = table_rows // 16 * 16
    table_s[0:whole] = stage_s[0:whole].astype(BF)
    rest = stage_s[whole:table_rows]
    table_s[whole : whole + 16] = jnp.concatenate(
        [rest, jnp.zeros((16 - (table_rows - whole), D), F32)], axis=0
    ).astype(BF)
    table_s[whole + 16 :] = jnp.zeros((TROWS - whole - 16, D), BF)
    for copy, place, targets in loads[1:]:
        copy.wait()
        for target, turned in targets:
            target[...] = (place[...].T if turned else place[...]).astype(BF)
    for copy in sends:
        copy.wait()
    codes = [codes_s[k] for k in range(4)]

    spread = (iota((STEPS, 512), 1) // CLASSES == iota((STEPS, 512), 0)).astype(F32).astype(BF)
    first = (iota((STEPS, 384), 0) == 0).astype(F32).astype(BF)
    class_lane = (iota((128, 512), 1) % CLASSES).astype(F32)
    lane = iota((128, 384), 1).astype(F32)
    for c in range(steps_all // 128):
        cols = slice(128 * c, 128 * c + 128)
        halves = []
        for k in range(2):
            hot = (dot_tn(codes[k][:, cols], spread) == class_lane).astype(F32).astype(BF)
            piece = dot_nn(hot, table_s[512 * k : 512 * k + 512]).astype(BF).astype(F32)
            halves.append(piece)
        hot = (dot_tn(codes[2][:, cols], first[:, :128]) == lane[:, :128]).astype(F32).astype(BF)
        action = dot_nn(hot, table_s[1024:1152]).astype(BF).astype(F32)
        hot = (dot_tn(codes[3][:, cols], first) + NA == lane).astype(F32).astype(BF)
        reward = dot_nn(hot, table_s[1024:1408]).astype(BF).astype(F32)
        pieces = [p.reshape(8, 1, STEPS, D) for p in (halves[0] + halves[1], action, reward)]
        x_s[0, 384 * c : 384 * c + 384] = jnp.concatenate(pieces, axis=1).reshape(384, D)
    for layer in range(LAYERS):
        rk = dot_nn(pos_ref[...], wsq_s[layer, 1]).astype(BF)
        for k in range(3):
            rk_s[layer, k] = expand(rk[TOKS * k : TOKS * k + TOKS])

    lane_hk = iota((TOKS, HK), 1) % TOKS
    key_step = lane_hk % STEPS
    key_time = 3 * key_step + lane_hk // STEPS
    row_tok = iota((TOKS, HK), 0)
    query_time = 3 * (row_tok % STEPS) + row_tok // STEPS
    causal = key_time <= query_time
    key_step_f = key_step.astype(F32)
    sum_hd = (iota((HK, D), 0) // TOKS == iota((HK, D), 1) // HD).astype(F32).astype(BF)
    sum_hk = (iota((D, HK), 0) // HD == iota((D, HK), 1) // TOKS).astype(F32).astype(BF)

    for layer in range(LAYERS):
        gain_a = small_ref[4 * layer : 4 * layer + 1]
        gain_b = small_ref[4 * layer + 1 : 4 * layer + 2]
        bias_u = small_ref[4 * layer + 2 : 4 * layer + 3]
        bias_v = small_ref[4 * layer + 3 : 4 * layer + 4]

        @pl.loop(0, chunks)
        def _(c):
            rows = pl.ds(pl.multiple_of(c * rows_c, rows_c), rows_c)
            x = x_s[layer, rows]
            low = (x * rms(x) * gain_a).astype(BF)
            a_s[layer, rows] = low
            q = dot_nn(low, wqkv_s[layer, :, :256]).astype(BF).astype(F32)
            qu = (q + bias_u).astype(BF)
            qv = (q + bias_v).astype(BF)
            key = dot_nn(low, wqkv_s[layer, :, 256:512]).astype(BF)
            val = dot_nn(low, wqkv_s[layer, :, 512:]).astype(BF)
            att_s[layer, rows, 0:256] = qu
            att_s[layer, rows, 256:512] = qv
            att_s[layer, rows, 512:768] = key
            att_s[layer, rows, 768:1024] = val
            qv4 = qv.reshape(CHUNK, 3, STEPS, D)
            place = [
                dot_nt(qv4[:, k].reshape(CHUNK * STEPS, D), rk_s[layer, k]) for k in range(3)
            ]
            start_c = start_s[pl.ds(c * CHUNK, CHUNK)]
            for b in range(CHUNK):
                span = slice(TOKS * b, TOKS * b + TOKS)
                score = dot_nt(qu[span], expand(key[span]))
                shifted = [
                    pltpu.roll(
                        place[k][STEPS * b : STEPS * b + STEPS],
                        HK - (STEPS - 1),
                        1,
                        stride=1,
                        stride_axis=0,
                    )
                    for k in range(3)
                ]
                begin = jnp.concatenate([start_c[b]] * 3, axis=0)
                begin = jnp.concatenate([begin] * 3, axis=1)
                score = (score + jnp.concatenate(shifted, axis=0)) * SCALE
                score = jnp.where(causal & (key_step_f >= begin), score, MASKED)
                probs = jnp.exp(score - segment_max(score)).astype(BF)
                pu_s[layer, pl.ds(pl.multiple_of(c * rows_c + TOKS * b, TOKS), TOKS)] = probs
                l_s[span] = dot_nn(probs, expand(val[span]))
            recip = 1.0 / dot_nn(pu_s[layer, rows], sum_hd)
            out = l_s[...] * recip
            o_s[layer, rows] = out
            mid = x + dot_nn(out.astype(BF), wsq_s[layer, 0])
            mid_s[layer, rows] = mid
            low = (mid * rms(mid) * gain_b).astype(BF)
            b_s[layer, rows] = low
            for j in range(FF // 256):
                cols = slice(256 * j, 256 * j + 256)
                inner = dot_nn(low, wup_s[layer, :, cols])
                square = inner * inner
                c0 = math.sqrt(2.0 / math.pi)
                tanh = jnp.tanh(c0 * inner * (1.0 + 0.044715 * square))
                half = 0.5 * (1.0 + tanh)
                hb_s[layer, rows, cols] = (inner * half).astype(BF)
                gp_s[layer, rows, cols] = (
                    half
                    + (0.5 * c0) * inner * (1.0 - tanh * tanh) * (1.0 + (3 * 0.044715) * square)
                ).astype(BF)
            nxt = mid + dot_nn(hb_s[layer, rows], wdown_s[layer])
            x_s[layer + 1, rows] = nxt

    gain_f = small_ref[4 * LAYERS : 4 * LAYERS + 1]
    xf = x_s[LAYERS].reshape(seqs, 3, STEPS, D)[:, 1].reshape(steps_all, D)
    feat = (xf * rms(xf) * gain_f).astype(BF)
    spread_t = (iota((512, STEPS), 0) // CLASSES == iota((512, STEPS), 1)).astype(F32).astype(BF)
    class_row = iota((4, CLASSES, steps_all), 1).astype(F32)
    loss = jnp.zeros((4, steps_all), F32)
    for k in range(2):
        follow_codes = pltpu.roll(codes[k].astype(F32), steps_all - 1, 1).astype(BF)
        for j in range(4):
            base = 512 * k + 128 * j
            logits = dot_nt(wheadt_s[base : base + 128], feat).reshape(4, CLASSES, steps_all)
            target = dot_nn(spread_t[128 * j : 128 * j + 128], follow_codes)
            hot = target.reshape(4, CLASSES, steps_all) == class_row
            top = jnp.max(logits, axis=1, keepdims=True)
            grown = jnp.exp(logits - top)
            total = jnp.sum(grown, axis=1, keepdims=True)
            picked = jnp.sum(jnp.where(hot, logits, 0.0), axis=1)
            loss = loss + valid_row * (jnp.log(total[:, 0]) + top[:, 0] - picked)
            slope = (grown * (1.0 / total) - jnp.where(hot, 1.0, 0.0)) * valid_row[None]
            slope_s[base : base + 128] = slope.reshape(128, steps_all).astype(BF)
    action_row = codes[2][0:1].astype(F32)
    discount_row = codes[2][1:2].astype(F32)
    reward_row = codes[3][0:1].astype(F32)
    logits = dot_nt(wheadt_s[1024:1280], feat)
    row = iota((256, steps_all), 0)
    hot = row == (reward_row + 1.0).astype(jnp.int32)
    disc = logits[:1]
    masked = jnp.where(row == 0, -3e38, logits)
    top = jnp.max(masked, axis=0, keepdims=True)
    grown = jnp.exp(masked - top)
    total = jnp.sum(grown, axis=0, keepdims=True)
    picked = jnp.sum(jnp.where(hot, logits, 0.0), axis=0, keepdims=True)
    fade = jnp.exp(-jnp.abs(disc))
    soft = jnp.maximum(disc, 0.0) + jnp.log(1.0 + fade)
    sigm = jnp.where(disc >= 0.0, 1.0, fade) / (1.0 + fade)
    loss_row = (
        jnp.sum(loss, axis=0, keepdims=True)
        + jnp.log(total)
        + top
        - picked
        + soft
        - discount_row * disc
    )
    slope = grown * (1.0 / total) - jnp.where(hot, 1.0, 0.0)
    slope = jnp.where(row == 0, sigm - discount_row, slope)
    slope_s[1024:1280] = slope.astype(BF)
    loss_sum = jnp.sum(loss_row)
    count = jnp.sum(valid_row) * CATS + 2.0 * steps_all
    slot_s[0, 9:10] = jnp.full((1, D), loss_sum, F32)
    slot_s[0, 10:11] = jnp.full((1, D), count, F32)
    slot_s[0, 11:16] = jnp.zeros((5, D), F32)

    feat_t = feat.astype(F32).T.astype(BF)
    for j in range(5):
        part = dot_nt(feat_t, slope_s[256 * j : 256 * j + 256])
        for k in range(2):
            base = 256 * (2 * j + k)
            g_s[base : base + 256] = part[:, 128 * k : 128 * k + 128].astype(BF)
    comm.open(0)
    dfeat = dot_nn(whead_s[...], slope_s[...]).T
    scale_f = rms(xf)
    hat = xf * scale_f
    slot_s[0, 8:9] = jnp.sum(dfeat * hat, axis=0, keepdims=True)
    inner = dfeat * gain_f
    dxf = scale_f * (inner - hat * jnp.mean(inner * hat, axis=-1, keepdims=True))
    gap = jnp.zeros((seqs, 1, STEPS, D), F32)
    x_s[LAYERS] = jnp.concatenate([gap, dxf.reshape(seqs, 1, STEPS, D), gap], axis=1).reshape(
        toks, D
    )

    for layer in reversed(range(LAYERS)):
        gain_a = small_ref[4 * layer : 4 * layer + 1]
        gain_b = small_ref[4 * layer + 1 : 4 * layer + 2]
        slot_s[0, 4 * layer : 4 * layer + 4] = jnp.zeros((4, D), F32)

        @pl.loop(0, chunks)
        def _(c):
            rows = pl.ds(pl.multiple_of(c * rows_c, rows_c), rows_c)
            comm.ticks(c, chunks)
            dy = x_s[LAYERS, rows]
            dyl = dy.astype(BF)
            dyl_s[rows] = dyl
            for j in range(FF // 256):
                cols = slice(256 * j, 256 * j + 256)
                dact = dot_nt(dyl, wdown_s[layer, cols])
                gp_s[layer, rows, cols] = (dact * gp_s[layer, rows, cols].astype(F32)).astype(BF)
            dlow = dot_nt(gp_s[layer, rows], wup_s[layer])
            mid = mid_s[layer, rows]
            scale = rms(mid)
            hat = mid * scale
            dgain = jnp.sum(dlow * hat, axis=0, keepdims=True)
            inner = dlow * gain_b
            dmid = scale * (inner - hat * jnp.mean(inner * hat, axis=-1, keepdims=True)) + dy
            slot_s[0, 4 * layer + 1 : 4 * layer + 2] += dgain
            mid_s[layer, rows] = dmid
            dml_s[rows] = dmid.astype(BF)

        base = 2560 + 6656 * (LAYERS - 1 - layer)

        def put(offset, value, base=base):
            size = value.shape[0]
            for k in range(2):
                at = base + offset + k * size
                g_s[at : at + size] = value[:, 128 * k : 128 * k + 128].astype(BF)

        for j in range(4):
            part = dot_tn(hb_s[layer, :, 256 * j : 256 * j + 256], dyl_s[...])
            for k in range(2):
                at = base + 1024 * k + 256 * j
                g_s[at : at + 256] = part[:, 128 * k : 128 * k + 128].astype(BF)
        comm.tick()
        for j in range(4):
            put(2048 + 512 * j, dot_tn(b_s[layer], gp_s[layer, :, 256 * j : 256 * j + 256]))
        comm.open(1 + 2 * (LAYERS - 1 - layer))

        @pl.loop(0, chunks)
        def _(c):
            rows = pl.ds(pl.multiple_of(c * rows_c, rows_c), rows_c)
            comm.ticks(c, chunks)
            dmid = mid_s[layer, rows]
            dml = dml_s[rows]
            recip = 1.0 / dot_nn(pu_s[layer, rows], sum_hd)
            do = dot_nt(dml, wsq_s[layer, 0]).astype(BF).astype(F32)
            do = (do * recip).astype(BF)
            mass = do.astype(F32) * o_s[layer, rows]
            mass_hi = mass.astype(BF)
            mass_lo = (mass - mass_hi.astype(F32)).astype(BF)
            delta = dot_nn(mass_hi, sum_hk) + dot_nn(mass_lo, sum_hk)
            qu = att_s[layer, rows, 0:256]
            key = att_s[layer, rows, 512:768]
            val = att_s[layer, rows, 768:1024]
            draws = []
            for b in range(CHUNK):
                span = slice(TOKS * b, TOKS * b + TOKS)
                probs = pu_s[layer, pl.ds(pl.multiple_of(c * rows_c + TOKS * b, TOKS), TOKS)]
                dprob = dot_nt(do[span], expand(val[span]))
                dscore = (probs.astype(F32) * (dprob - delta[span])).astype(BF)
                wide = dscore.astype(F32)
                draws.append(
                    [unskew(wide[STEPS * k : STEPS * k + STEPS]).astype(BF) for k in range(3)]
                )
                dval = fold(dot_tn(probs, do[span])).astype(BF)
                dkey = (fold(dot_tn(dscore, qu[span])) * SCALE).astype(BF)
                l_s[span] = dot_nn(dscore, expand(key[span])) * SCALE
                out_rows = pl.ds(pl.multiple_of(c * rows_c + TOKS * b, TOKS), TOKS)
                pu_s[layer, out_rows] = jnp.concatenate(draws[b], axis=0)
                att_s[layer, out_rows, 512:768] = dkey
                att_s[layer, out_rows, 768:1024] = dval
            dqv = [
                dot_nn(
                    jnp.concatenate([draws[b][k] for b in range(CHUNK)], axis=0), rk_s[layer, k]
                ).reshape(CHUNK, 1, STEPS, D)
                for k in range(3)
            ]
            dqv = jnp.concatenate(dqv, axis=1).reshape(rows_c, D) * SCALE
            dqu = l_s[...]
            slot_s[0, 4 * layer + 2 : 4 * layer + 3] += jnp.sum(dqu, axis=0, keepdims=True)
            slot_s[0, 4 * layer + 3 : 4 * layer + 4] += jnp.sum(dqv, axis=0, keepdims=True)
            dq = (dqu + dqv).astype(BF)
            att_s[layer, rows, 0:256] = dq
            dlow = (
                dot_nt(dq, wqkv_s[layer, :, :256])
                + dot_nt(att_s[layer, rows, 512:768], wqkv_s[layer, :, 256:512])
                + dot_nt(att_s[layer, rows, 768:1024], wqkv_s[layer, :, 512:])
            )
            x = x_s[layer, rows]
            scale = rms(x)
            hat = x * scale
            slot_s[0, 4 * layer : 4 * layer + 1] += jnp.sum(dlow * hat, axis=0, keepdims=True)
            inner = dlow * gain_a
            dx = scale * (inner - hat * jnp.mean(inner * hat, axis=-1, keepdims=True)) + dmid
            x_s[LAYERS, rows] = dx

        comm.tick()
        put(4096, dot_tn(o_s[layer].astype(BF), dml_s[...]))
        drk = []
        draw = pu_s[layer].reshape(seqs, 3, STEPS, HK)
        qv = att_s[layer, :, 256:512].reshape(seqs, 3, STEPS, D)
        for k in range(3):
            wide = dot_tn(
                draw[:, k].reshape(steps_all, HK), qv[:, k].reshape(steps_all, D)
            )
            drk.append(fold(wide) * SCALE)
        put(4608, dot_tn(pos_ref[...], jnp.concatenate(drk, axis=0).astype(BF)))
        put(5120, dot_tn(a_s[layer], att_s[layer, :, 0:256]))
        put(5632, dot_tn(a_s[layer], att_s[layer, :, 512:768]))
        put(6144, dot_tn(a_s[layer], att_s[layer, :, 768:1024]))
        if layer:
            comm.open(2 * (LAYERS - layer))

    dtok = x_s[LAYERS].reshape(seqs, 3, STEPS, D).astype(BF)
    dtok = [dtok[:, k].reshape(steps_all, D) for k in range(3)]
    base = 2560 + 6656 * LAYERS
    class_row = (iota((256, steps_all), 0) % CLASSES).astype(F32)
    for k in range(2):
        for j in range(2):
            wide = dot_nn(spread_t[256 * j : 256 * j + 256], codes[k])
            hot = (wide == class_row).astype(F32).astype(BF)
            part = dot_nn(hot, dtok[0])
            for h in range(2):
                at = base + 1280 * h + 512 * k + 256 * j
                g_s[at : at + 256] = part[:, 128 * h : 128 * h + 128].astype(BF)
    row = iota((288, steps_all), 0)
    hot_a = (row == action_row.astype(jnp.int32)).astype(F32).astype(BF)
    hot_r = (row == (reward_row + NA).astype(jnp.int32)).astype(F32).astype(BF)
    part = dot_nn(hot_a, dtok[1]) + dot_nn(hot_r, dtok[2])
    for h in range(2):
        at = base + 1280 * h + 1024
        g_s[at : at + 256] = part[:256, 128 * h : 128 * h + 128].astype(BF)
    slot_s[0, 16:40] = part[256:280]
    comm.finish(slot_s, got_s, extra_sems, total_ref)


def run_step(codes, seg, pos, small, weights, streams, groups):
    seqs = codes.shape[0] // streams
    toks = seqs * TOKS
    plan, recv, own = exchange_plan(streams, groups)
    rounds = len(plan[0][0]["order"])
    vmem, dma = pltpu.VMEM, pltpu.SemaphoreType.DMA
    hbm = pl.BlockSpec(memory_space=pl.ANY)
    table, qkv, square, up, down, head = weights
    return pl.pallas_call(
        lambda *refs: step_kernel(streams, groups, *refs),
        out_shape=(
            jax.ShapeDtypeStruct((sum(SECTIONS), 128), BF),
            jax.ShapeDtypeStruct((40, D), F32),
        ),
        in_specs=[hbm] + [pl.BlockSpec(memory_space=vmem)] * 3 + [hbm] * 6,
        out_specs=[hbm, pl.BlockSpec(memory_space=vmem)],
        scratch_shapes=[
            vmem((LAYERS + 1, toks, D), F32),
            vmem((LAYERS, toks, 1024), BF),
            vmem((LAYERS, toks, HK), BF),
            vmem((LAYERS, toks, D), F32),
            vmem((LAYERS, toks, D), F32),
            vmem((LAYERS, toks, FF), BF),
            vmem((LAYERS, toks, FF), BF),
            vmem((LAYERS, toks, D), BF),
            vmem((LAYERS, toks, D), BF),
            vmem((toks, D), BF),
            vmem((toks, D), BF),
            vmem((LAYERS, 3, HK, D), BF),
            vmem((seqs, STEPS, 128), F32),
            vmem((CHUNK * TOKS, D), F32),
            vmem((HCOLS, seqs * STEPS), BF),
            vmem((TROWS, D), BF),
            vmem(qkv.shape, BF),
            vmem(square.shape, BF),
            vmem(up.shape, BF),
            vmem(down.shape, BF),
            vmem(head.shape, BF),
            vmem(head.shape[::-1], BF),
            vmem(table.shape, F32),
            vmem(codes.shape, jnp.int32),
            vmem((streams, STEPS, seqs * STEPS), BF),
            vmem((streams, STEPS, seqs * STEPS), BF),
            vmem((sum(SECTIONS), 128), BF),
            vmem((recv, 128), BF),
            vmem((own, 128), BF),
            vmem((rounds + 1, 40, D), F32),
            vmem((rounds, 40, D), F32),
            dma((2 + 13 * LAYERS + 5,)),
            dma((2, streams - 1)),
            dma((len(plan), 3, 4, rounds)),
            dma((len(plan), 3)),
            dma((2, rounds)),
        ],
        compiler_params=pltpu.CompilerParams(
            collective_id=0, has_side_effects=True, vmem_limit_bytes=VMEM_LIMIT
        ),
        name="step",
    )(codes, seg, pos, small, table, qkv, square, up, down, head)


def update_pieces():
    pieces = []
    for k in range(LAYERS):
        layer = LAYERS - 1 - k
        base = 2560 + 6656 * k
        for half in range(2):
            r = 512 * half
            pieces.append(
                (4, (layer,), r, 512, [(base + 1024 * j + r, 128 * j) for j in range(2)])
            )
        pieces.append((3, (layer,), 0, 256, [(base + 2048 + 256 * j, 128 * j) for j in range(8)]))
        pieces.append((2, (layer, 0), 0, 256, [(base + 4096 + 256 * j, 128 * j) for j in range(2)]))
        pieces.append((2, (layer, 1), 0, 256, [(base + 4608 + 256 * j, 128 * j) for j in range(2)]))
        pieces.append((1, (layer,), 0, 256, [(base + 5120 + 256 * j, 128 * j) for j in range(6)]))
    pieces.append((6, (), 0, 256, [(256 * j, 128 * j) for j in range(10)]))
    base = 2560 + 6656 * LAYERS
    pieces.append((0, (), 0, 1280, [(base + 1280 * j, 128 * j) for j in range(2)]))
    return pieces


def update_kernel(clip_value, step_rate, *refs):
    g_ref, e_ref = refs[:2]
    ins = refs[2:23]
    stat_ref = refs[23]
    outs = refs[24:45]
    bufs = refs[45:66]
    isem, osem = refs[66:]
    pieces = update_pieces()
    table_rows = ins[0].shape[0]
    tail = table_rows - 1280

    def view(ref, piece):
        array, lead, first, rows, _ = piece
        if lead:
            ref = ref.at[lead]
        if ref.shape[0] == rows:
            return ref
        return ref.at[pl.ds(first, rows)]

    def transfer(kind, n, k, piece):
        src, dst = (ins, bufs) if kind == 0 else (bufs, outs)
        array = piece[0]
        sem = (isem, osem)[kind].at[k, n]
        return pltpu.make_async_copy(
            view(src[7 * k + array], piece), view(dst[7 * k + array], piece), sem
        )

    specials = [(0, (), 1280, tail, None), (5, (), 0, ins[5].shape[0], None)]
    order = specials + pieces
    for n, piece in enumerate(order):
        for k in range(3):
            transfer(0, n, k, piece).start()

    block = 128
    count = g_ref.shape[0] // block

    def gather(j, total):
        v = g_ref[pl.ds(pl.multiple_of(j * block, block), block)].astype(F32)
        return total + jnp.sum((v * v).reshape(block // 8, 8, 128), axis=0)

    total = lax.fori_loop(0, count, gather, jnp.zeros((8, 128), F32))
    rest = jnp.sum(e_ref[0:9] * e_ref[0:9]) + jnp.sum(e_ref[16:40] * e_ref[16:40])
    loss = jnp.max(e_ref[9:10])
    terms = jnp.max(e_ref[10:11])
    inverse = 1.0 / jnp.full((8, 128), terms, F32)
    norm = jnp.sqrt(jnp.full((8, 128), jnp.sum(total) + rest, F32)) * inverse
    factor = inverse * clip_value / jnp.maximum(norm, clip_value)
    stat_ref[0:8] = jnp.full((8, 128), loss, F32)
    stat_ref[8:16] = jnp.full((8, 128), terms, F32)
    stat_ref[16:24] = norm
    factor = factor[:1]

    def advance(views, rows, cols, gradient, scale):
        w, m, e = [v[rows, cols] for v in views]
        clipped = gradient * scale
        moment = MOMENTUM_RATE * m + clipped
        weight = w - step_rate * (clipped + MOMENTUM_RATE * moment)
        views[0][rows, cols] = weight
        views[1][rows, cols] = moment
        views[2][rows, cols] = AVERAGE_RATE * e + (1.0 - AVERAGE_RATE) * weight

    for n, piece in enumerate(order):
        array, lead, first, rows, blocks = piece
        for k in range(3):
            transfer(0, n, k, piece).wait()
        views = [bufs[7 * k + array].at[lead] if lead else bufs[7 * k + array] for k in range(3)]
        if blocks is None:
            at = 16 if array == 0 else 0
            wide = jnp.concatenate([factor, factor], axis=1)
            advance(
                views, slice(first, first + rows), slice(0, D), e_ref[at : at + rows], wide
            )
        else:
            step = 64

            @pl.loop(0, rows // step)
            def _(j):
                for source, column in blocks:
                    g = g_ref[pl.ds(pl.multiple_of(source + j * step, step), step)].astype(F32)
                    at = pl.ds(pl.multiple_of(first + j * step, step), step)
                    advance(views, at, slice(column, column + 128), g, factor)

        for k in range(3):
            transfer(1, n, k, piece).start()
    for n, piece in enumerate(order):
        for k in range(3):
            transfer(1, n, k, piece).wait()


def update_all(grads, extra, arrays, clip_value, step_rate):
    vmem = pltpu.VMEM
    count = len(update_pieces()) + 2
    hbm = pl.BlockSpec(memory_space=pl.ANY)
    results = pl.pallas_call(
        lambda *refs: update_kernel(clip_value, step_rate, *refs),
        out_shape=[jax.ShapeDtypeStruct((24, 128), F32)]
        + [jax.ShapeDtypeStruct(a.shape, F32) for a in arrays],
        in_specs=[pl.BlockSpec(memory_space=vmem)] * 2 + [hbm] * 21,
        out_specs=[pl.BlockSpec(memory_space=vmem)] + [hbm] * 21,
        scratch_shapes=[vmem(a.shape, F32) for a in arrays]
        + [pltpu.SemaphoreType.DMA((3, count)), pltpu.SemaphoreType.DMA((3, count))],
        compiler_params=pltpu.CompilerParams(vmem_limit_bytes=44 * 1000 * 1000),
        name="update",
    )(grads, extra, *arrays)
    return results[0], results[1:]


def on_device(step_codes, segments, *arrays):
    streams = lax.axis_size("stream")
    groups = lax.axis_size("seq")
    group_seqs = step_codes.shape[0]
    table, qkv, square, up, down, small, head = arrays[:7]
    pos = jnp.asarray(position_rows()).astype(BF)
    grads, extra = run_step(
        step_codes, segments, pos, small, (table, qkv, square, up, down, head), streams, groups
    )
    params_total = sum(w.size for w in arrays[:7])
    clip_value = CLIP_SCALE * (group_seqs * groups * STEPS) ** (-0.5)
    step_rate = STEP_SCALE * params_total**0.5 / clip_value
    stats, updated = update_all(grads, extra, arrays, clip_value, step_rate)
    return (stats[0, 0], stats[8, 0], stats[16, 0], *updated)


def solution(mesh):
    return jax.shard_map(
        on_device,
        mesh=mesh,
        in_specs=(P("seq", None, "stream"), P("seq", None)) + (P(),) * 21,
        out_specs=(P(),) * 24,
        check_vma=False,
    )
```

time: 207 us -> 197 us (0.952)
  Pallas kernels: 174 us -> 183 us
  local copies, waits for them, and re-layouts: 20.9 us -> 12.7 us
  other arithmetic: 6.37 us -> 0 us
  starting transfers between devices: 4.24 us -> 0 us
    pallas_call x2 -> x1, Pallas kernels: 157 us -> 166 us  [run_step(): pl.pallas_call(lambda *refs: step_kernel(streams, groups, *refs), out_sha...]
    convert_element_type x5 -> x0, other arithmetic: 5.39 us -> none  [the longest x1 2.17 us: on_device(): square.astype(BF)]
    all_to_all x1 -> x0, starting transfers between devices: 4.24 us -> none  [on_device(): lax.all_to_all(step_codes.reshape(streams, own, STEPS, -1), 'stream', spl...]
    unnamed x44 -> x28, local copies, waits for them, and re-layouts: 16.3 us -> 12.2 us
  transfers between devices with their start and end apart: 1 -> 0, of which waited for: 0 -> 0; matrix products, arithmetic and copies ran while one was open for 4% -> 0% of each run, Pallas kernels for 0% -> 0%
where the time goes in v1:
time: 197 us; the launch traced here: 196 us
  Pallas kernels  183 us (93%)
  local copies, waits for them, and re-layouts  12.7 us (6%)
    pallas_call x1, Pallas kernels, run_step(): pl.pallas_call(lambda *refs: step_kernel(streams, groups, *refs), out_sha...  166 us
    pallas_call x1, Pallas kernels, update_all(): pl.pallas_call(lambda *refs: update_kernel(clip_value, step_rate, *refs),...  17.2 us
    unnamed x28, local copies, waits for them, and re-layouts  12.2 us

profile of v1, /device:TPU:0, one launch (start us, length us, event | category | flops | bytes accessed | tf_op | source)
XLA Modules:
  0.0 196.4 jit_solution(18281822115520694536)
XLA Ops:
  0.7 1.4 copy.49.refs_1_
  2.1 2.3 %copy.48.refs_0_ = s32[128,16,16]{2,1,0:T(8,128)} copy(s32[128,16,16]{0,2,1:T(8,128)} %param.24) | data formatting | bytes 262144 | tf_op args[0]
  4.4 0.0 copy-start
  4.4 0.0 copy-start.1
  4.4 0.0 copy-start.2
  4.4 0.0 copy-start.11
  4.4 0.0 copy-start.12
  4.4 165.8 %step.1 = (bf16[18432,128]{1,0:T(8,128)(2,1)}, f32[40,256]{1,0:T(8,128)}) custom-call(s32[128,16,16]{2,1,0:T(8,128)} %copy.48.refs_0_, s32[128,16]{1,0:T(8,128)} %copy.49.refs_1_, bf16[144,256]{1,0:T(8,128)(2,1)} %constant.3.refs_2_, f32[9,256]{1,0:T(8,128)} %refs_7_.3, f32[1297,256]{1,0:T(8,128)} %refs_2_.1, f32[2,256,768]{2,1,0:T(8,128)} %refs_3_.3, ...), custom_call_target="tpu_custom_call" | custom-call | tf_op jit(solution)/shard_map/step/pallas_call | solution.py:805
  170.2 0.0 copy-done
  170.2 0.0 copy-done.1
  170.2 0.0 copy-done.2
  170.2 0.0 copy-done.9
  170.2 0.0 copy-done.11
  170.2 0.0 copy-done.12
  170.2 0.0 copy-start.3
  170.2 1.3 copy-done.3
  171.5 1.3 copy-done.4
  172.9 1.3 copy-done.5
  174.2 1.3 copy-done.6
  175.5 1.2 copy-done.7
  176.7 1.2 copy-done.8
  178.0 0.8 copy-done.10
  178.7 17.2 %update.1 = (f32[24,128]{1,0:T(8,128)S(1)}, f32[1297,256]{1,0:T(8,128)}, f32[2,256,768]{2,1,0:T(8,128)}, f32[2,2,256,256]{3,2,1,0:T(8,128)}, f32[2,256,1024]{2,1...) custom-call(bf16[18432,128]{1,0:T(8,128)(2,1)} %get-tuple-element.48, ...), custom_call_target="tpu_custom_call" | custom-call | tf_op jit(solution)/shard_map/update/pallas_call | solution.py:971
  195.9 0.5 fusion
  (7 shorter events, 0.0 us)
Async XLA Ops:
  4.4 165.8 %copy-start = (f32[1297,256]{1,0:T(8,128)S(1)}, f32[1297,256]{1,0:T(8,128)}, u32[]{:S(2)}) copy-start(f32[1297,256]{1,0:T(8,128)} %refs_2_.1) | copy-start | bytes 3984388
  4.4 165.8 %copy-start.1 = (f32[256,1280]{1,0:T(8,128)S(1)}, f32[256,1280]{1,0:T(8,128)}, u32[]{:S(2)}) copy-start(f32[256,1280]{1,0:T(8,128)} %refs_8_.3) | copy-start | bytes 3932164
  4.4 165.8 %copy-start.2 = (f32[2,2,256,256]{3,2,1,0:T(8,128)S(1)}, f32[2,2,256,256]{3,2,1,0:T(8,128)}, u32[]{:S(2)}) copy-start(f32[2,2,256,256]{3,2,1,0:T(8,128)} %refs_4_.3) | copy-start | bytes 3145732
  4.4 165.8 %copy-start.9 = (f32[9,256]{1,0:T(8,128)S(1)}, f32[9,256]{1,0:T(8,128)}, u32[]{:S(2)}) copy-start(f32[9,256]{1,0:T(8,128)} %refs_7_.3) | copy-start | bytes 27652
  4.4 165.8 %copy-start.11 = (f32[9,256]{1,0:T(8,128)S(1)}, f32[9,256]{1,0:T(8,128)}, u32[]{:S(2)}) copy-start(f32[9,256]{1,0:T(8,128)} %refs_14_.1) | copy-start | bytes 27652
  4.4 165.8 %copy-start.12 = (f32[9,256]{1,0:T(8,128)S(1)}, f32[9,256]{1,0:T(8,128)}, u32[]{:S(2)}) copy-start(f32[9,256]{1,0:T(8,128)} %refs_21_.1) | copy-start | bytes 27652
  170.2 1.3 copy-start.3
  171.5 1.3 copy-start.4
  172.9 1.3 copy-start.5
  174.2 1.3 copy-start.6
  175.5 1.2 copy-start.7
  176.7 1.2 copy-start.8
  177.9 0.8 copy-start.10
